TPU v7x, 128 devices: a whole 4x4x4 slice. The times are simulated.
128 devices in a mesh: grp: 4 (over x_lo, core), sub: 32 (over y, z, x_hi).
Axes of the slice: x: 4 (x_hi: 2, x_lo: 2; x = x_hi * 2 + x_lo), y: 4, z: 4, core: 2. Of those that a mesh axis runs over, the one named last changes fastest.
Arguments:
- states: bfloat16 [524288, 128], P(('grp', 'sub')), may hold values from -6 to 6
- cotangent: bfloat16 [524288, 128], P(('grp', 'sub')), may hold values from -6 to 6
- fine_self: bfloat16 [128, 128], replicated, may hold values from -0.5 to 0.5
- fine_other: bfloat16 [128, 128], replicated, may hold values from -0.5 to 0.5
- fine_node: bfloat16 [128, 128], replicated, may hold values from -0.375 to 0.375
- coarse_self: bfloat16 [128, 128], replicated, may hold values from -0.5 to 0.5
- coarse_other: bfloat16 [128, 128], replicated, may hold values from -0.5 to 0.5
- coarse_node: bfloat16 [128, 128], replicated, may hold values from -0.375 to 0.375
- prolong: bfloat16 [128, 128], replicated, may hold values from -0.5 to 0.5
- fine_nbr: int32 [524288, 8], P(('grp', 'sub')), may hold values from 0 to 5119, as said below
- fine_mask: int32 [524288, 8], P(('grp', 'sub')), may hold values 0 or 1
- fine_send_lo: int32 [65536], P(('grp', 'sub')), may hold values from 0 to 4095
- fine_send_hi: int32 [65536], P(('grp', 'sub')), may hold values from 0 to 4095
- coarse_nbr: int32 [32768, 8], P('sub'), may hold values from 0 to 1151, as said below
- coarse_mask: int32 [32768, 8], P('sub'), may hold values 0 or 1
- coarse_send_lo: int32 [2048], P('sub'), may hold values from 0 to 1023
- coarse_send_hi: int32 [2048], P('sub'), may hold values from 0 to 1023
- coarse_owner: int32 [524288], P(('grp', 'sub')), may hold values from 0 to 1023, as said below
Outputs:
- result: bfloat16 [524288, 128], P(('grp', 'sub'))
- grad_states: bfloat16 [524288, 128], P(('grp', 'sub'))
- grad_weights: float32 [7, 128, 128], replicated
Inputs may be any that keep to these rules, and one draw needn't show every extreme that they name: `coarse_owner`: on the devices of grp index 0 every mid-level cell is named by exactly 4096 // 1024 fine cells of that device; elsewhere names are drawn freely. `fine_nbr`: with B = 64, local row r of a device lies in block b = r // B; each of its slots names a row of block b of the local rows (b * B to b * B + B - 1), or row 4096 + (b % 8) * B + j, or row 4608 + (b % 8) * B + j, for some j below B. `coarse_nbr`: local row r of a partition lies in block b = r // 64; each of its slots names a row of block b of the local rows, or any of the 128 halo rows of the table.
All inputs are finite; a program needn't handle non-finite values. No bound on the sum of `fine_mask` or of `coarse_mask` on one device may be relied on, other than what follows from the above.
Results may differ from a plain program's by a relative error of at most 0.015.
Values may be sent and summed in bfloat16 or wider, within the bound.
A program may use at most 128 MiB of HBM per device.

v0:
```python
import math

import jax
import jax.numpy as jnp
from jax import lax
from jax.sharding import PartitionSpec as P

highest = lax.Precision.HIGHEST


def shifted(block, axis, distance):
    devices = range(lax.axis_size(axis))
    route = [(i - distance, i) for i in devices if i - distance in devices]
    return lax.ppermute(block, axis, route)


def halo_table(far_term, send_lo, send_hi):
    from_lower = shifted(far_term[send_hi], "sub", 1)
    from_upper = shifted(far_term[send_lo], "sub", -1)
    return jnp.concatenate([far_term, from_lower, from_upper], 0)


def block_layout(neighbours, rows, halo_rows, halo_blocks):
    block_rows = halo_rows // halo_blocks
    blocks = rows // block_rows
    block_index = (jnp.arange(rows, dtype=jnp.int32) // block_rows)[:, None]
    halo_index = block_index % halo_blocks
    columns = jnp.where(
        neighbours < rows,
        neighbours - block_index * block_rows,
        jnp.where(
            neighbours < rows + halo_rows,
            block_rows + neighbours - rows - halo_index * block_rows,
            2 * block_rows + neighbours - rows - halo_rows - halo_index * block_rows,
        ),
    )
    group_blocks = math.gcd(blocks, max(1, 1024 // block_rows))
    return (columns, block_rows, blocks, group_blocks)


def block_windows(table, rows, halo_rows, halo_blocks, block_rows, blocks):
    features = table.shape[1]
    local_part = table[:rows].reshape(blocks // halo_blocks, halo_blocks, block_rows, features)
    lower_part = jnp.broadcast_to(
        table[rows : rows + halo_rows].reshape(1, halo_blocks, block_rows, features),
        local_part.shape,
    )
    upper_part = jnp.broadcast_to(
        table[rows + halo_rows :].reshape(1, halo_blocks, block_rows, features), local_part.shape
    )
    return jnp.concatenate([local_part, lower_part, upper_part], 2).reshape(
        blocks, 3 * block_rows, features
    )


def one_hot_rows(column_block, block_rows):
    group_blocks = column_block.shape[0]
    flat_columns = column_block.reshape(group_blocks, -1)
    return flat_columns[..., None] == jnp.arange(3 * block_rows, dtype=jnp.int32)[None, None, :]


def level_forward(
    latents, w_self, w_other, w_node, neighbours, in_use, send_lo, send_hi, halo_blocks
):
    rows, features = latents.shape
    slots = neighbours.shape[1]
    halo_rows = send_lo.shape[0]
    own_term = jnp.dot(latents, w_self, preferred_element_type=jnp.float32)
    far_term = jnp.dot(latents, w_other, preferred_element_type=jnp.float32).astype(jnp.bfloat16)
    table = halo_table(far_term, send_lo, send_hi)
    columns, block_rows, blocks, group_blocks = block_layout(
        neighbours, rows, halo_rows, halo_blocks
    )
    windows = block_windows(table, rows, halo_rows, halo_blocks, block_rows, blocks)
    steps = blocks // group_blocks

    def advance(carry, piece):
        own_block, column_block, use_block, window_block = piece
        selector = one_hot_rows(column_block, block_rows).astype(jnp.bfloat16)
        picked = jnp.einsum(
            "grc,gcd->grd", selector, window_block, preferred_element_type=jnp.float32
        ).reshape(group_blocks, block_rows, slots, features)
        preact = own_block[:, :, None, :] + picked
        summed_block = (jax.nn.silu(preact) * use_block[..., None].astype(jnp.float32)).sum(2)
        return (carry, summed_block.astype(jnp.bfloat16))

    _, summed = lax.scan(
        advance,
        None,
        (
            own_term.reshape(steps, group_blocks, block_rows, features),
            columns.reshape(steps, group_blocks, block_rows, slots),
            in_use.reshape(steps, group_blocks, block_rows, slots),
            windows.reshape(steps, group_blocks, 3 * block_rows, features),
        ),
    )
    summed = summed.reshape(rows, features)
    updated = latents.astype(jnp.float32) + jnp.dot(
        summed, w_node, preferred_element_type=jnp.float32
    )
    return (updated, own_term, table, summed)


def level_backward(
    latents,
    w_self,
    w_other,
    w_node,
    own_term,
    table,
    summed,
    neighbours,
    in_use,
    send_lo,
    send_hi,
    grad_up,
    halo_blocks,
):
    rows, features = latents.shape
    slots = neighbours.shape[1]
    halo_rows = send_lo.shape[0]
    columns, block_rows, blocks, group_blocks = block_layout(
        neighbours, rows, halo_rows, halo_blocks
    )
    windows = block_windows(table, rows, halo_rows, halo_blocks, block_rows, blocks)
    steps = blocks // group_blocks
    grad_sum = jnp.dot(grad_up, w_node.astype(jnp.float32).T, precision=highest)
    grad_node = jnp.dot(summed.astype(jnp.float32).T, grad_up, precision=highest)

    def advance(carry, piece):
        own_block, column_block, use_block, window_block, grad_block = piece
        selector = one_hot_rows(column_block, block_rows)
        picked = jnp.einsum(
            "grc,gcd->grd",
            selector.astype(jnp.bfloat16),
            window_block,
            preferred_element_type=jnp.float32,
        ).reshape(group_blocks, block_rows, slots, features)
        preact = own_block[:, :, None, :] + picked
        gate_value = jax.nn.sigmoid(preact)
        slope = gate_value * (1.0 + preact * (1.0 - gate_value))
        grad_pre = grad_block[:, :, None, :] * use_block[..., None].astype(jnp.float32) * slope
        grad_window = jnp.einsum(
            "grc,grd->gcd",
            selector.astype(jnp.float32),
            grad_pre.reshape(group_blocks, block_rows * slots, features),
            precision=highest,
        )
        return (carry, (grad_pre.sum(2), grad_window))

    _, (grad_own, grad_windows) = lax.scan(
        advance,
        None,
        (
            own_term.reshape(steps, group_blocks, block_rows, features),
            columns.reshape(steps, group_blocks, block_rows, slots),
            in_use.reshape(steps, group_blocks, block_rows, slots),
            windows.reshape(steps, group_blocks, 3 * block_rows, features),
            grad_sum.reshape(steps, group_blocks, block_rows, features),
        ),
    )
    grad_own = grad_own.reshape(rows, features)
    grad_windows = grad_windows.reshape(
        blocks // halo_blocks, halo_blocks, 3 * block_rows, features
    )
    grad_local = grad_windows[:, :, :block_rows].reshape(rows, features)
    grad_lower = grad_windows[:, :, block_rows : 2 * block_rows].sum(0).reshape(halo_rows, features)
    grad_upper = grad_windows[:, :, 2 * block_rows :].sum(0).reshape(halo_rows, features)
    back_up = shifted(grad_upper.astype(jnp.bfloat16), "sub", 1).astype(grad_upper.dtype)
    back_down = shifted(grad_lower.astype(jnp.bfloat16), "sub", -1).astype(grad_lower.dtype)
    grad_far = (
        grad_local
        + jax.ops.segment_sum(back_up, send_lo, num_segments=rows)
        + jax.ops.segment_sum(back_down, send_hi, num_segments=rows)
    )
    latent_f = latents.astype(jnp.float32)
    grad_self = jnp.dot(latent_f.T, grad_own, precision=highest)
    grad_other = jnp.dot(latent_f.T, grad_far, precision=highest)
    grad_latent = (
        grad_up
        + jnp.dot(grad_own, w_self.astype(jnp.float32).T, precision=highest)
        + jnp.dot(grad_far, w_other.astype(jnp.float32).T, precision=highest)
    )
    return (grad_latent, grad_self, grad_other, grad_node)


def per_device(
    states,
    cotangent,
    fine_self,
    fine_other,
    fine_node,
    coarse_self,
    coarse_other,
    coarse_node,
    prolong,
    fine_nbr,
    fine_mask,
    fine_send_lo,
    fine_send_hi,
    coarse_nbr,
    coarse_mask,
    coarse_send_lo,
    coarse_send_hi,
    coarse_owner,
):
    coarse_rows = coarse_nbr.shape[0]
    updated, own_term, table, summed = level_forward(
        states, fine_self, fine_other, fine_node, fine_nbr, fine_mask, fine_send_lo, fine_send_hi, 8
    )
    part_totals = jax.ops.segment_sum(updated, coarse_owner, num_segments=coarse_rows)
    part_counts = jax.ops.segment_sum(
        jnp.ones(coarse_owner.shape[0], jnp.float32), coarse_owner, num_segments=coarse_rows
    )
    totals, counts = lax.psum((part_totals, part_counts), "grp")
    coarse_in = (totals / counts[:, None]).astype(jnp.bfloat16)
    coarse_up, coarse_own, coarse_table, coarse_sum = level_forward(
        coarse_in,
        coarse_self,
        coarse_other,
        coarse_node,
        coarse_nbr,
        coarse_mask,
        coarse_send_lo,
        coarse_send_hi,
        1,
    )
    coarse_out = coarse_up.astype(jnp.bfloat16)
    picked = coarse_out[coarse_owner]
    result = (updated + jnp.dot(picked, prolong, preferred_element_type=jnp.float32)).astype(
        jnp.bfloat16
    )
    grad_out = cotangent.astype(jnp.float32)
    grad_prolong = jnp.dot(picked.astype(jnp.float32).T, grad_out, precision=highest)
    grad_picked = jnp.dot(grad_out, prolong.astype(jnp.float32).T, precision=highest)
    grad_coarse = lax.psum(
        jax.ops.segment_sum(grad_picked, coarse_owner, num_segments=coarse_rows).astype(
            jnp.bfloat16
        ),
        "grp",
    ).astype(jnp.float32)
    grad_cin, grad_cself, grad_cother, grad_cnode = level_backward(
        coarse_in,
        coarse_self,
        coarse_other,
        coarse_node,
        coarse_own,
        coarse_table,
        coarse_sum,
        coarse_nbr,
        coarse_mask,
        coarse_send_lo,
        coarse_send_hi,
        grad_coarse,
        1,
    )
    grad_updated = grad_out + (grad_cin / counts[:, None])[coarse_owner]
    grad_latent, grad_fself, grad_fother, grad_fnode = level_backward(
        states,
        fine_self,
        fine_other,
        fine_node,
        own_term,
        table,
        summed,
        fine_nbr,
        fine_mask,
        fine_send_lo,
        fine_send_hi,
        grad_updated,
        8,
    )
    grad_weights = lax.psum(
        jnp.stack(
            [
                grad_fself,
                grad_fother,
                grad_fnode,
                0.25 * grad_cself,
                0.25 * grad_cother,
                0.25 * grad_cnode,
                grad_prolong,
            ]
        ),
        ("grp", "sub"),
    )
    return (result, grad_latent.astype(jnp.bfloat16), grad_weights)


def solution(mesh):
    in_specs = (
        P(("grp", "sub"), None),
        P(("grp", "sub"), None),
        P(),
        P(),
        P(),
        P(),
        P(),
        P(),
        P(),
        P(("grp", "sub"), None),
        P(("grp", "sub"), None),
        P(("grp", "sub")),
        P(("grp", "sub")),
        P("sub", None),
        P("sub", None),
        P("sub"),
        P("sub"),
        P(("grp", "sub")),
    )
    out_specs = (P(("grp", "sub"), None), P(("grp", "sub"), None), P())
    return jax.shard_map(
        per_device, mesh=mesh, in_specs=in_specs, out_specs=out_specs, check_vma=False
    )
```

profile of v0, /device:TPU:1, one launch (start us, length us, event | category | flops | bytes accessed | tf_op | source)
XLA Modules:
  0.0 544.8 jit_solution(17477605065782601686)
XLA Ops:
  15.0 6.9 %collective-permute-start = (bf16[512,128]{1,0:T(8,128)(2,1)}, bf16[512,128]{1,0:T(8,128)(2,1)}, u32[]{:S(2)}, u32[]{:S(2)}) collective-permute-start(bf16[512,128]{1,0:T(8,128)(2,1)} %gather_fusion), channel_id=1, source_target_pairs={{0,1},{1,2},{2,3},{3,4},{4,5},{5,6},{6,7},{7,8},{8,9},{9,10},{10,1... | collective-permute-start | bytes 393224 | tf_op jit(solution)/shard_map/ppermute | solution.py:14
  23.7 22.8 %scatter_custom_fusion.2 = f32[1024,128]{1,0:T(8,128)S(1)} fusion(s32[4096]{0:T(1024)} %param.39, f32[4096,128]{1,0:T(8,128)} %fusion.100, f32[]{:T(128)} %constant.189.clone.1), kind=kCustom, calls=%fused_computation.131 | custom fusion | flops 524288 | bytes 524800 | tf_op jit(solution)/shard_map/scatter-add | solution.py:237
  56.7 46.1 %while.4 = (s32[]{:T(128)}, bf16[4,16,64,128]{3,2,1,0:T(8,128)(2,1)}, f32[4,16,64,128]{3,2,1,0:T(8,128)}, s32[4,16,64,8]{1,3,2,0:T(8,128)}, bf16[4,16,192,128]{3...) while((s32[]{:T(128)}, bf16[4,16,64,128]{3,2,1,0:T(8,128)(2,1)}, f32[4,16,64,128]{3,2,1,0:T(8,128)}, ...), condition=%wide.region_2.3_spmd, body=%wide.region_0.2_spmd.sunk | while | flops 411443200 | bytes 3539049 | solution.py:87
  60.0 7.5 %multiply_reduce_fusion.6 = bf16[16,64,128]{2,1,0:T(8,128)(2,1)S(1)} fusion(f32[16,64,8]{2,1,0:T(8,128)S(1)} %convert_bitcast_fusion.5, f32[16,64,128]{2,1,0:T(8,128)S(1)} %dynamic-slice_bitcast_fusion.9, s32[16,512]{1,0:T(8,128)S(1)} %copy.76, bf16[4,16,192,128]{3,2,1,0:T(8,128)(2,1)} %get-tuple-element.317, s32[]{:T(128)S(6)} %copy.86), kind=kOutput, calls=%fused_computation.14.clone.1 | convolution fusion | flops 411435008 | bytes 1638404 | tf_op jit(solution)/shard_map/while/body/eval_jaxpr/grc,gcd->grd/dot_general | solution.py:80
  71.5 7.5 %multiply_reduce_fusion.6 = bf16[16,64,128]{2,1,0:T(8,128)(2,1)S(1)} fusion(f32[16,64,8]{2,1,0:T(8,128)S(1)} %convert_bitcast_fusion.5, f32[16,64,128]{2,1,0:T(8,128)S(1)} %dynamic-slice_bitcast_fusion.9, s32[16,512]{1,0:T(8,128)S(1)} %copy.76, bf16[4,16,192,128]{3,2,1,0:T(8,128)(2,1)} %get-tuple-element.317, s32[]{:T(128)S(6)} %copy.86), kind=kOutput, calls=%fused_computation.14.clone.1 | convolution fusion | flops 411435008 | bytes 1638404 | tf_op jit(solution)/shard_map/while/body/eval_jaxpr/grc,gcd->grd/dot_general | solution.py:80
  83.0 7.5 %multiply_reduce_fusion.6 = bf16[16,64,128]{2,1,0:T(8,128)(2,1)S(1)} fusion(f32[16,64,8]{2,1,0:T(8,128)S(1)} %convert_bitcast_fusion.5, f32[16,64,128]{2,1,0:T(8,128)S(1)} %dynamic-slice_bitcast_fusion.9, s32[16,512]{1,0:T(8,128)S(1)} %copy.76, bf16[4,16,192,128]{3,2,1,0:T(8,128)(2,1)} %get-tuple-element.317, s32[]{:T(128)S(6)} %copy.86), kind=kOutput, calls=%fused_computation.14.clone.1 | convolution fusion | flops 411435008 | bytes 1638404 | tf_op jit(solution)/shard_map/while/body/eval_jaxpr/grc,gcd->grd/dot_general | solution.py:80
  94.5 7.5 %multiply_reduce_fusion.6 = bf16[16,64,128]{2,1,0:T(8,128)(2,1)S(1)} fusion(f32[16,64,8]{2,1,0:T(8,128)S(1)} %convert_bitcast_fusion.5, f32[16,64,128]{2,1,0:T(8,128)S(1)} %dynamic-slice_bitcast_fusion.9, s32[16,512]{1,0:T(8,128)S(1)} %copy.76, bf16[4,16,192,128]{3,2,1,0:T(8,128)(2,1)} %get-tuple-element.317, s32[]{:T(128)S(6)} %copy.86), kind=kOutput, calls=%fused_computation.14.clone.1 | convolution fusion | flops 411435008 | bytes 1638404 | tf_op jit(solution)/shard_map/while/body/eval_jaxpr/grc,gcd->grd/dot_general | solution.py:80
  104.5 23.1 %scatter_custom_fusion = f32[1024,128]{1,0:T(8,128)} fusion(s32[4096]{0:T(1024)S(1)} %copy-done.39, f32[4096,128]{1,0:T(8,128)S(1)} %convolution_add_fusion.3, f32[]{:T(128)} %constant.189.clone.1), kind=kCustom, calls=%fused_computation.133 | custom fusion | flops 524288 | bytes 524292 | tf_op jit(solution)/shard_map/scatter-add | solution.py:211
  128.6 28.8 %scatter_custom_fusion.1 = f32[1024]{0:T(1024)S(1)} fusion(s32[4096]{0:T(1024)S(1)} %copy-done.39, f32[4096]{0:T(1024)S(1)} %broadcast.258, f32[]{:T(128)} %constant.189.clone.1), kind=kCustom, calls=%fused_computation.174 | custom fusion | flops 4096 | bytes 4100 | tf_op jit(solution)/shard_map/scatter-add | solution.py:212
  158.8 6.4 %psum.29 = f32[1024]{0:T(1024)S(1)} all-reduce(f32[1024]{0:T(1024)S(1)} %scatter_custom_fusion.1), channel_id=1, replica_groups=mesh['grp'=4,'sub'=32] {'grp'}, use_global_device_ids=true, to_apply=%region_6.7 | all-reduce | flops 1024 | bytes 8192 | tf_op jit(solution)/shard_map/psum | solution.py:215
  167.2 4.3 all-reduce.4.cloned.1.call-done
  173.7 11.3 %collective-permute-start.3 = (bf16[64,128]{1,0:T(8,128)(2,1)S(1)}, bf16[64,128]{1,0:T(8,128)(2,1)S(1)}, u32[]{:S(2)}, u32[]{:S(2)}) collective-permute-start(bf16[64,128]{1,0:T(8,128)(2,1)S(1)} %gather_fusion.3), channel_id=1, source_target_pairs={{1,0},{2,1},{3,2},{4,3},{5,4},{6,5},{7,6},{8,7},{9,8},{10,9},{11,1... | collective-permute-start | bytes 49160 | tf_op jit(solution)/shard_map/ppermute | solution.py:14
  185.8 5.5 %collective-permute-start.2 = (bf16[64,128]{1,0:T(8,128)(2,1)S(1)}, bf16[64,128]{1,0:T(8,128)(2,1)S(1)}, u32[]{:S(2)}, u32[]{:S(2)}) collective-permute-start(bf16[64,128]{1,0:T(8,128)(2,1)S(1)} %gather_fusion.2), channel_id=1, source_target_pairs={{0,1},{1,2},{2,3},{3,4},{4,5},{5,6},{6,7},{7,8},{8,9},{9,10},{10,1... | collective-permute-start | bytes 49160 | tf_op jit(solution)/shard_map/ppermute | solution.py:14
  192.2 8.2 %multiply_reduce_fusion.2 = (f32[16,64,128]{2,1,0:T(8,128)}, bf16[16,64,128]{2,1,0:T(8,128)(2,1)S(1)}, f32[16,512,128]{2,1,0:T(8,128)}) fusion(f32[16,64,128]{2,1,0:T(8,128)} %bitcast.230, f32[16,64,8]{2,1,0:T(8,128)S(1)} %bitcast.223, f32[16,64,128]{2,1,0:T(8,128)S(1)} %bitcast.232, bf16[16,1,64,128]{3,2,0,1:T(8,128)(2,1)S(1)} %broadcast_in_dim.146, ...), kind=kOutput, calls=%fused_computation.80 | convolution fusion | flops 421003264 | bytes 6881280 | tf_op jit(solution)/shard_map/while/body/eval_jaxpr/grc,gcd->grd/dot_general | solution.py:80
  201.4 12.1 %gather_fusion.4 = bf16[4096,128]{1,0:T(8,128)(2,1)S(1)} fusion(bf16[1024,128]{1,0:T(8,128)(2,1)S(1)} %fusion.53, s32[4096]{0:T(1024)S(1)} %fusion.88), kind=kCustom, calls=%fused_computation.4 | custom fusion | bytes 2113536 | tf_op jit(solution)/shard_map/gather | solution.py:229
  215.6 6.8 %fusion.49 = f32[16,1,192,128]{3,2,0,1:T(8,128)S(1)} fusion(f32[16,512,128]{2,1,0:T(8,128)} %get-tuple-element.194, f32[16,512]{1,0:T(8,128)S(1)} %copy-done.35, f32[16,64,128]{2,1,0:T(8,128)S(1)} %bitcast.231, f32[16,64,128]{2,1,0:T(8,128)S(1)} %bitcast.233, s32[16,512]{1,0:T(8,128)S(1)} %eq.72), kind=kOutput, calls=%fused_computation.93 | convolution fusion | flops 2427977728 | bytes 6881280 | tf_op jit(solution)/shard_map/while/body/eval_jaxpr/grc,grd->gcd/dot_general | solution.py:143
  223.8 6.1 %collective-permute-start.4 = (bf16[64,128]{1,0:T(8,128)(2,1)S(1)}, bf16[64,128]{1,0:T(8,128)(2,1)S(1)}, u32[]{:S(2)}, u32[]{:S(2)}) collective-permute-start(bf16[64,128]{1,0:T(8,128)(2,1)S(1)} %get-tuple-element.156), channel_id=1, source_target_pairs={{0,1},{1,2},{2,3},{3,4},{4,5},{5,6},{6,7},{7,8},{8,9},{9,10},{10,1... | collective-permute-start | bytes 49160 | tf_op jit(solution)/shard_map/ppermute | solution.py:14
  233.6 10.8 %gather_fusion.5 = f32[4096,128]{1,0:T(8,128)S(1)} fusion(f32[1024,128]{1,0:T(8,128)S(1)} %fusion.52, s32[4096]{0:T(1024)S(1)} %fusion.88), kind=kCustom, calls=%fused_computation.5 | custom fusion | bytes 4210688 | tf_op jit(solution)/shard_map/gather | solution.py:257
  248.1 91.3 %while.5 = (s32[]{:T(128)}, f32[4,16,64,128]{3,2,1,0:T(8,128)}, f32[4,16,192,128]{3,2,1,0:T(8,128)}, f32[4,16,64,128]{3,2,1,0:T(8,128)}, s32[4,16,64,8]{2,1,0,3:...) while((s32[]{:T(128)}, f32[4,16,64,128]{3,2,1,0:T(8,128)}, ...), condition=%wide.region_16.17_spmd, body=%wide.region_14.16_spmd.sunk | while | flops 2843615232 | bytes 19726488 | solution.py:151
  253.5 8.7 %multiply_reduce_fusion.7 = (f32[16,64,128]{2,1,0:T(8,128)S(1)}, f32[16,512,128]{2,1,0:T(8,128)}) fusion(f32[16,64,128]{2,1,0:T(8,128)S(1)} %get-tuple-element.293, f32[16,64,8]{2,1,0:T(8,128)} %copy.78, f32[16,64,128]{2,1,0:T(8,128)} %get-tuple-element.295, bf16[4,16,192,128]{3,2,1,0:T(8,128)(2,1)} %get-tuple-element.345, s32[]{:T(128)S(6)} %copy.96, ...), kind=kOutput, calls=%fused_computation.39.clone.1 | convolution fusion | flops 415629312 | bytes 7110660 | tf_op jit(solution)/shard_map/while/body/eval_jaxpr/grc,gcd->grd/dot_general | solution.py:133
  263.2 7.7 %bitcast_dynamic-update-slice_fusion.8 = f32[4,16,192,128]{3,2,1,0:T(8,128)} fusion(f32[4,16,192,128]{3,2,1,0:T(8,128)} %get-tuple-element.331, s32[]{:T(128)S(6)} %copy.96, f32[16,512,128]{2,1,0:T(8,128)} %get-tuple-element.297, f32[16,512]{1,0:T(8,128)S(1)} %copy.80, f32[16,64,128]{2,1,0:T(8,128)S(1)} %get-tuple-element.293, ...), kind=kOutput, calls=%fused_computation.46.clone.1 | convolution fusion | flops 2427977728 | bytes 6881284 | tf_op jit(solution)/shard_map/while/body/eval_jaxpr/grc,grd->gcd/dot_general | solution.py:143
  276.4 8.7 %multiply_reduce_fusion.7 = (f32[16,64,128]{2,1,0:T(8,128)S(1)}, f32[16,512,128]{2,1,0:T(8,128)}) fusion(f32[16,64,128]{2,1,0:T(8,128)S(1)} %get-tuple-element.293, f32[16,64,8]{2,1,0:T(8,128)} %copy.78, f32[16,64,128]{2,1,0:T(8,128)} %get-tuple-element.295, bf16[4,16,192,128]{3,2,1,0:T(8,128)(2,1)} %get-tuple-element.345, s32[]{:T(128)S(6)} %copy.96, ...), kind=kOutput, calls=%fused_computation.39.clone.1 | convolution fusion | flops 415629312 | bytes 7110660 | tf_op jit(solution)/shard_map/while/body/eval_jaxpr/grc,gcd->grd/dot_general | solution.py:133
  286.1 7.7 %bitcast_dynamic-update-slice_fusion.8 = f32[4,16,192,128]{3,2,1,0:T(8,128)} fusion(f32[4,16,192,128]{3,2,1,0:T(8,128)} %get-tuple-element.331, s32[]{:T(128)S(6)} %copy.96, f32[16,512,128]{2,1,0:T(8,128)} %get-tuple-element.297, f32[16,512]{1,0:T(8,128)S(1)} %copy.80, f32[16,64,128]{2,1,0:T(8,128)S(1)} %get-tuple-element.293, ...), kind=kOutput, calls=%fused_computation.46.clone.1 | convolution fusion | flops 2427977728 | bytes 6881284 | tf_op jit(solution)/shard_map/while/body/eval_jaxpr/grc,grd->gcd/dot_general | solution.py:143
  299.2 8.7 %multiply_reduce_fusion.7 = (f32[16,64,128]{2,1,0:T(8,128)S(1)}, f32[16,512,128]{2,1,0:T(8,128)}) fusion(f32[16,64,128]{2,1,0:T(8,128)S(1)} %get-tuple-element.293, f32[16,64,8]{2,1,0:T(8,128)} %copy.78, f32[16,64,128]{2,1,0:T(8,128)} %get-tuple-element.295, bf16[4,16,192,128]{3,2,1,0:T(8,128)(2,1)} %get-tuple-element.345, s32[]{:T(128)S(6)} %copy.96, ...), kind=kOutput, calls=%fused_computation.39.clone.1 | convolution fusion | flops 415629312 | bytes 7110660 | tf_op jit(solution)/shard_map/while/body/eval_jaxpr/grc,gcd->grd/dot_general | solution.py:133
  308.9 7.7 %bitcast_dynamic-update-slice_fusion.8 = f32[4,16,192,128]{3,2,1,0:T(8,128)} fusion(f32[4,16,192,128]{3,2,1,0:T(8,128)} %get-tuple-element.331, s32[]{:T(128)S(6)} %copy.96, f32[16,512,128]{2,1,0:T(8,128)} %get-tuple-element.297, f32[16,512]{1,0:T(8,128)S(1)} %copy.80, f32[16,64,128]{2,1,0:T(8,128)S(1)} %get-tuple-element.293, ...), kind=kOutput, calls=%fused_computation.46.clone.1 | convolution fusion | flops 2427977728 | bytes 6881284 | tf_op jit(solution)/shard_map/while/body/eval_jaxpr/grc,grd->gcd/dot_general | solution.py:143
  322.0 8.7 %multiply_reduce_fusion.7 = (f32[16,64,128]{2,1,0:T(8,128)S(1)}, f32[16,512,128]{2,1,0:T(8,128)}) fusion(f32[16,64,128]{2,1,0:T(8,128)S(1)} %get-tuple-element.293, f32[16,64,8]{2,1,0:T(8,128)} %copy.78, f32[16,64,128]{2,1,0:T(8,128)} %get-tuple-element.295, bf16[4,16,192,128]{3,2,1,0:T(8,128)(2,1)} %get-tuple-element.345, s32[]{:T(128)S(6)} %copy.96, ...), kind=kOutput, calls=%fused_computation.39.clone.1 | convolution fusion | flops 415629312 | bytes 7110660 | tf_op jit(solution)/shard_map/while/body/eval_jaxpr/grc,gcd->grd/dot_general | solution.py:133
  331.7 7.7 %bitcast_dynamic-update-slice_fusion.8 = f32[4,16,192,128]{3,2,1,0:T(8,128)} fusion(f32[4,16,192,128]{3,2,1,0:T(8,128)} %get-tuple-element.331, s32[]{:T(128)S(6)} %copy.96, f32[16,512,128]{2,1,0:T(8,128)} %get-tuple-element.297, f32[16,512]{1,0:T(8,128)S(1)} %copy.80, f32[16,64,128]{2,1,0:T(8,128)S(1)} %get-tuple-element.293, ...), kind=kOutput, calls=%fused_computation.46.clone.1 | convolution fusion | flops 2427977728 | bytes 6881284 | tf_op jit(solution)/shard_map/while/body/eval_jaxpr/grc,grd->gcd/dot_general | solution.py:143
  339.4 4.5 convolution_add_fusion.1
  347.2 6.8 %collective-permute-start.6 = (bf16[512,128]{1,0:T(8,128)(2,1)S(1)}, bf16[512,128]{1,0:T(8,128)(2,1)S(1)}, u32[]{:S(2)}, u32[]{:S(2)}) collective-permute-start(bf16[512,128]{1,0:T(8,128)(2,1)S(1)} %bitcast.234), channel_id=1, source_target_pairs={{0,1},{1,2},{2,3},{3,4},{4,5},{5,6},{6,7},{7,8},{8,9},{9,10},{10,1... | collective-permute-start | bytes 393224 | tf_op jit(solution)/shard_map/ppermute | solution.py:14
  356.5 9.9 %scatter_custom_fusion.4 = f32[4096,128]{1,0:T(8,128)} fusion(f32[4096,128]{1,0:T(8,128)} %bitcast.213, s32[1024]{0:T(1024)} %bitcast.239, bf16[512,128]{1,0:T(8,128)(2,1)S(1)} %collective-permute-done.7, bf16[]{:T(256)} %constant.201, bf16[512,128]{1,0:T(8,128)(2,1)S(1)} %collective-permute-done.6), kind=kCustom, calls=%fused_computation.125 | custom fusion | flops 655360 | bytes 2359808 | tf_op jit(solution)/shard_map/add | solution.py:172
  366.5 4.2 fusion.60
  382.9 153.1 %all-reduce.8.cloned.1.call-done = f32[7,128,128]{1,2,0:T(8,128)} async-done(((f32[7,128,128]{1,2,0:T(8,128)}), f32[7,128,128]{1,2,0:T(8,128)}) %all-reduce.8.cloned.1.call-update) | async-done | bytes 458768 | tf_op jit(solution)/shard_map/psum | solution.py:273
  (239 shorter events, 102.4 us)
Async XLA Ops:
  7.2 14.8 %copy-start = (bf16[128,128]{1,0:T(8,128)(2,1)S(1)}, bf16[128,128]{1,0:T(8,128)(2,1)}, u32[]{:S(2)}) copy-start(bf16[128,128]{1,0:T(8,128)(2,1)} %param.30) | copy-start | bytes 98308
  7.2 158.0 %all-reduce.6.cloned.1.call-start = ((), (), s32[]{:S(2)}) async-start(), calls=%async_computation.1 | async-start | bytes 524288 | tf_op jit(solution)/shard_map/psum | solution.py:236
  8.7 38.6 %copy-start.1 = (bf16[4096,128]{1,0:T(8,128)(2,1)S(1)}, bf16[4096,128]{1,0:T(8,128)(2,1)}, u32[]{:S(2)}) copy-start(bf16[4096,128]{1,0:T(8,128)(2,1)} %param.22) | copy-start | bytes 3145732
  8.7 38.6 %copy-start.25 = (bf16[128,128]{1,0:T(8,128)(2,1)S(1)}, bf16[128,128]{1,0:T(8,128)(2,1)}, u32[]{:S(2)}) copy-start(bf16[128,128]{1,0:T(8,128)(2,1)} %param.24) | copy-start | bytes 98308
  11.8 41.6 %collective-permute-start.1 = (bf16[512,128]{1,0:T(8,128)(2,1)S(1)}, bf16[512,128]{1,0:T(8,128)(2,1)S(1)}, u32[]{:S(2)}, u32[]{:S(2)}) collective-permute-start(bf16[512,128]{1,0:T(8,128)(2,1)S(1)} %gather_fusion.1), channel_id=1, source_target_pairs={{1,0},{2,1},{3,2},{4,3},{5,4},{6,5},{7,6},{8,7},{9,8},{10,9},{11,1... | collective-permute-start | bytes 393224 | tf_op jit(solution)/shard_map/ppermute | solution.py:14
  15.0 34.1 %copy-start.42 = (s32[64]{0:T(128)S(1)}, s32[64]{0:T(128)}, u32[]{:S(2)}) copy-start(s32[64]{0:T(128)} %param.37) | copy-start | bytes 772
  15.0 34.1 %copy-start.44 = (s32[64]{0:T(128)S(1)}, s32[64]{0:T(128)}, u32[]{:S(2)}) copy-start(s32[64]{0:T(128)} %param.38) | copy-start | bytes 772
  15.0 34.9 %copy-start.40 = (s32[512]{0:T(512)S(1)}, s32[512]{0:T(512)}, u32[]{:S(2)}) copy-start(s32[512]{0:T(512)} %param.33) | copy-start | bytes 6148
  15.0 34.9 %copy-start.41 = (s32[512]{0:T(512)S(1)}, s32[512]{0:T(512)}, u32[]{:S(2)}) copy-start(s32[512]{0:T(512)} %param.34) | copy-start | bytes 6148
  15.0 38.4 %collective-permute-start = (bf16[512,128]{1,0:T(8,128)(2,1)}, bf16[512,128]{1,0:T(8,128)(2,1)}, u32[]{:S(2)}, u32[]{:S(2)}) collective-permute-start(bf16[512,128]{1,0:T(8,128)(2,1)} %gather_fusion), channel_id=1, source_target_pairs={{0,1},{1,2},{2,3},{3,4},{4,5},{5,6},{6,7},{7,8},{8,9},{9,10},{10,1... | collective-permute-start | bytes 393224 | tf_op jit(solution)/shard_map/ppermute | solution.py:14
  23.7 26.2 %copy-start.30 = (s32[4096,8]{0,1:T(8,128)S(1)}, s32[4096,8]{0,1:T(8,128)}, u32[]{:S(2)}) copy-start(s32[4096,8]{0,1:T(8,128)} %param.31) | copy-start | bytes 393220
  23.7 28.3 %copy-start.28 = (s32[4096,8]{0,1:T(8,128)S(1)}, s32[4096,8]{0,1:T(8,128)}, u32[]{:S(2)}) copy-start(s32[4096,8]{0,1:T(8,128)} %param.32) | copy-start | bytes 393220
  47.2 124.2 %all-reduce.4.cloned.1.call-start = ((), (), s32[]{:S(2)}) async-start(), calls=%async_computation | async-start | bytes 1048576 | tf_op jit(solution)/shard_map/psum | solution.py:215
  56.7 46.1 %copy-start.24 = (bf16[128,128]{1,0:T(8,128)(2,1)S(1)}, bf16[128,128]{1,0:T(8,128)(2,1)}, u32[]{:S(2)}) copy-start(bf16[128,128]{1,0:T(8,128)(2,1)} %param.26) | copy-start | bytes 98308
  102.8 25.0 %copy-start.43 = (s32[64]{0:T(128)S(1)}, s32[64]{0:T(128)}, u32[]{:S(2)}) copy-start(s32[64]{0:T(128)} %param.37) | copy-start | bytes 772
  102.8 25.0 %copy-start.45 = (s32[64]{0:T(128)S(1)}, s32[64]{0:T(128)}, u32[]{:S(2)}) copy-start(s32[64]{0:T(128)} %param.38) | copy-start | bytes 772
  102.8 25.7 %copy-start.36 = (s32[1024,8]{0,1:T(8,128)S(1)}, s32[1024,8]{0,1:T(8,128)}, u32[]{:S(2)}) copy-start(s32[1024,8]{0,1:T(8,128)} %param.36) | copy-start | bytes 98308
  102.8 62.4 %copy-start.29 = (bf16[128,128]{1,0:T(8,128)(2,1)S(1)}, bf16[128,128]{1,0:T(8,128)(2,1)}, u32[]{:S(2)}) copy-start(bf16[128,128]{1,0:T(8,128)(2,1)} %param.29) | copy-start | bytes 98308
  102.8 69.9 %copy-start.33 = (bf16[128,128]{1,0:T(8,128)(2,1)S(1)}, bf16[128,128]{1,0:T(8,128)(2,1)}, u32[]{:S(2)}) copy-start(bf16[128,128]{1,0:T(8,128)(2,1)} %param.28) | copy-start | bytes 98308
  102.8 88.5 %copy-start.31 = (bf16[128,128]{1,0:T(8,128)(2,1)S(1)}, bf16[128,128]{1,0:T(8,128)(2,1)}, u32[]{:S(2)}) copy-start(bf16[128,128]{1,0:T(8,128)(2,1)} %param.27) | copy-start | bytes 98308
  127.7 408.3 %all-reduce.8.cloned.1.call-start = ((), (), s32[]{:S(2)}) async-start(), calls=%async_computation.2 | async-start | bytes 917504 | tf_op jit(solution)/shard_map/psum | solution.py:273
  165.1 27.1 %copy-start.37 = (f32[1024]{0:T(1024)}, f32[1024]{0:T(1024)S(1)}, u32[]{:S(2)}) copy-start(f32[1024]{0:T(1024)S(1)} %psum.29) | copy-start | bytes 12292
  172.7 27.8 %copy-start.7 = (bf16[1024,128]{1,0:T(8,128)(2,1)}, bf16[1024,128]{1,0:T(8,128)(2,1)S(1)}, u32[]{:S(2)}) copy-start(bf16[1024,128]{1,0:T(8,128)(2,1)S(1)} %divide_convert_fusion) | copy-start | bytes 786436
  173.7 17.8 %collective-permute-start.3 = (bf16[64,128]{1,0:T(8,128)(2,1)S(1)}, bf16[64,128]{1,0:T(8,128)(2,1)S(1)}, u32[]{:S(2)}, u32[]{:S(2)}) collective-permute-start(bf16[64,128]{1,0:T(8,128)(2,1)S(1)} %gather_fusion.3), channel_id=1, source_target_pairs={{1,0},{2,1},{3,2},{4,3},{5,4},{6,5},{7,6},{8,7},{9,8},{10,9},{11,1... | collective-permute-start | bytes 49160 | tf_op jit(solution)/shard_map/ppermute | solution.py:14
  185.8 6.3 %collective-permute-start.2 = (bf16[64,128]{1,0:T(8,128)(2,1)S(1)}, bf16[64,128]{1,0:T(8,128)(2,1)S(1)}, u32[]{:S(2)}, u32[]{:S(2)}) collective-permute-start(bf16[64,128]{1,0:T(8,128)(2,1)S(1)} %gather_fusion.2), channel_id=1, source_target_pairs={{0,1},{1,2},{2,3},{3,4},{4,5},{5,6},{6,7},{7,8},{8,9},{9,10},{10,1... | collective-permute-start | bytes 49160 | tf_op jit(solution)/shard_map/ppermute | solution.py:14
  215.6 17.7 %copy-start.34 = (bf16[128,128]{1,0:T(8,128)(2,1)S(1)}, bf16[128,128]{1,0:T(8,128)(2,1)}, u32[]{:S(2)}) copy-start(bf16[128,128]{1,0:T(8,128)(2,1)} %param.28) | copy-start | bytes 98308
  215.6 17.7 %copy-start.38 = (f32[1024]{0:T(1024)S(1)}, f32[1024]{0:T(1024)}, u32[]{:S(2)}) copy-start(f32[1024]{0:T(1024)} %copy-done.37) | copy-start | bytes 12292
  222.5 7.9 %collective-permute-start.5 = (bf16[64,128]{1,0:T(8,128)(2,1)S(1)}, bf16[64,128]{1,0:T(8,128)(2,1)S(1)}, u32[]{:S(2)}, u32[]{:S(2)}) collective-permute-start(bf16[64,128]{1,0:T(8,128)(2,1)S(1)} %get-tuple-element.157), channel_id=1, source_target_pairs={{1,0},{2,1},{3,2},{4,3},{5,4},{6,5},{7,6},{8,7},{9,8},{10,9},{11,1... | collective-permute-start | bytes 49160 | tf_op jit(solution)/shard_map/ppermute | solution.py:14
  223.8 7.0 %collective-permute-start.4 = (bf16[64,128]{1,0:T(8,128)(2,1)S(1)}, bf16[64,128]{1,0:T(8,128)(2,1)S(1)}, u32[]{:S(2)}, u32[]{:S(2)}) collective-permute-start(bf16[64,128]{1,0:T(8,128)(2,1)S(1)} %get-tuple-element.156), channel_id=1, source_target_pairs={{0,1},{1,2},{2,3},{3,4},{4,5},{5,6},{6,7},{7,8},{8,9},{9,10},{10,1... | collective-permute-start | bytes 49160 | tf_op jit(solution)/shard_map/ppermute | solution.py:14
  248.1 91.3 %copy-start.26 = (bf16[128,128]{1,0:T(8,128)(2,1)S(1)}, bf16[128,128]{1,0:T(8,128)(2,1)}, u32[]{:S(2)}) copy-start(bf16[128,128]{1,0:T(8,128)(2,1)} %param.24) | copy-start | bytes 98308
  345.9 10.6 %collective-permute-start.7 = (bf16[512,128]{1,0:T(8,128)(2,1)S(1)}, bf16[512,128]{1,0:T(8,128)(2,1)S(1)}, u32[]{:S(2)}, u32[]{:S(2)}) collective-permute-start(bf16[512,128]{1,0:T(8,128)(2,1)S(1)} %bitcast.235), channel_id=1, source_target_pairs={{1,0},{2,1},{3,2},{4,3},{5,4},{6,5},{7,6},{8,7},{9,8},{10,9},{11,1... | collective-permute-start | bytes 393224 | tf_op jit(solution)/shard_map/ppermute | solution.py:14
  347.2 9.3 %collective-permute-start.6 = (bf16[512,128]{1,0:T(8,128)(2,1)S(1)}, bf16[512,128]{1,0:T(8,128)(2,1)S(1)}, u32[]{:S(2)}, u32[]{:S(2)}) collective-permute-start(bf16[512,128]{1,0:T(8,128)(2,1)S(1)} %bitcast.234), channel_id=1, source_target_pairs={{0,1},{1,2},{2,3},{3,4},{4,5},{5,6},{6,7},{7,8},{8,9},{9,10},{10,1... | collective-permute-start | bytes 393224 | tf_op jit(solution)/shard_map/ppermute | solution.py:14
  (28 other events, 231.7 us)
Sparse Core Ops, SparseCore 0:
  47.4 42.0 all-reduce.5
  127.8 43.5 all-reduce.3
  379.3 156.5 all-reduce.7
where the time goes:
time: 555 us; the launch traced here: 545 us
  waiting for transfers between devices  158 us (28%)
  matrix products  149 us (27%)
  other arithmetic  96.8 us (17%)
  local copies, waits for them, and re-layouts  78.2 us (14%)
  starting transfers between devices  40.7 us (7%)
  between operations  14.8 us (3%)
  blocking collectives  6.36 us (1%)
    psum x1, waiting for transfers between devices, per_device(): lax.psum(jnp.stack([grad_fself, grad_fother, grad_fnode, 0.25 * grad_csel...  153 us
    ppermute x8, starting transfers between devices, shifted(): return lax.ppermute(block, axis, route)  40.6 us
    dot_general x5, matrix products, advance(): jnp.einsum('grc,gcd->grd', selector, window_block, preferred_element_type...  38.2 us
    dot_general x5, matrix products, advance(): jnp.einsum('grc,grd->gcd', selector.astype(jnp.float32), grad_pre.reshape...  37.6 us
    dot_general x4, matrix products, advance(): jnp.einsum('grc,gcd->grd', selector.astype(jnp.bfloat16), window_block, p...  35 us
    scatter-add x1, other arithmetic, per_device(): jax.ops.segment_sum(jnp.ones(coarse_owner.shape[0], jnp.float32), coarse_...  28.8 us
    scatter-add x1, other arithmetic, per_device(): jax.ops.segment_sum(updated, coarse_owner, num_segments=coarse_rows)  23.1 us
    scatter-add x1, other arithmetic, per_device(): jax.ops.segment_sum(grad_picked, coarse_owner, num_segments=coarse_rows)  22.8 us
  transfers between devices with their start and end apart: 11, of which 4 were waited for; matrix products, arithmetic and copies ran while one was open for 27% of the time, Pallas kernels for 0%

commit v1 on v0

v1 whole, which is shorter than its diff:
```python
import functools

import jax
import jax.numpy as jnp
from jax import lax
from jax.experimental import pallas as pl
from jax.experimental.pallas import tpu as pltpu
from jax.sharding import PartitionSpec as P

MESH = pl.DeviceIdType.MESH
BF = jnp.bfloat16
F32 = jnp.float32
D = 128
BLK = 64
TILE = 512


def dot(a, b, ca=1, cb=0):
    return lax.dot_general(a, b, (((ca,), (cb,)), ((), ())), preferred_element_type=F32)


def rows_at(start, size):
    return pl.ds(pl.multiple_of(start, size if size % 8 == 0 else 8), size)


def spread(row, rows):
    one = jnp.broadcast_to(row, (16, row.shape[1])).astype(BF)
    return jnp.concatenate([one] * (rows // 16), axis=0)


def iota_bf(rows, lanes, base=0):
    return (lax.broadcasted_iota(jnp.int32, (rows, lanes), 0) + base).astype(F32).astype(BF)


def one_hot(row, rows, base=0):
    hit = iota_bf(rows, row.shape[1], base) == spread(row, rows)
    return jnp.where(hit, jnp.ones((), BF), jnp.zeros((), BF))


def group_hot(values, group):
    inside = jnp.where((values >> 8) == group, values & 255, -1).astype(F32)
    return one_hot(inside, 256)


def prepare_slots(nbr, msk, cidx, rows, halo, halo_blocks):
    def body(p, carry):
        v = nbr[:, rows_at(p * 128, 128)]
        used = msk[:, rows_at(p * 128, 128)] > 0
        lane = lax.broadcasted_iota(jnp.int32, (8, 128), 1)
        slot = lax.broadcasted_iota(jnp.int32, (8, 128), 0)
        blk = 2 * p + (lane >> 6)
        hblk = blk & (halo_blocks - 1)
        col = jnp.where(
            v < rows,
            v - blk * BLK,
            jnp.where(v < rows + halo, v - rows - hblk * BLK + BLK, v - rows - halo - hblk * BLK + 2 * BLK),
        )
        col = jnp.where(used, col, -1)
        own = jnp.where(used, 3 * BLK + (lane & (BLK - 1)), -1)
        first = lane < BLK

        def halves(x):
            later = pltpu.roll(x, 4, 0)
            return (
                jnp.where(first, x, pltpu.roll(later, BLK, 1)),
                jnp.where(first, pltpu.roll(x, BLK, 1), later),
            )

        for half, (c, o) in enumerate(zip(halves(col), halves(own))):
            cidx[2 * p + half] = jnp.where(slot < 4, c, pltpu.roll(o, 4, 0)).astype(F32)
        return carry

    lax.fori_loop(0, rows // 128, body, 0)


def build_selectors(cidx, sel, blocks):
    def body(b, carry):
        idx = cidx[b]
        for j in range(4):
            sel[b, 0 : 3 * BLK, j * 128 : (j + 1) * 128] = one_hot(idx[j : j + 1], 3 * BLK)
            sel[b, 3 * BLK : 4 * BLK, j * 128 : (j + 1) * 128] = one_hot(idx[4 + j : 5 + j], BLK, 3 * BLK)
        return carry

    lax.fori_loop(0, blocks, body, 0)


def gather_rows(index, source, staged, start, count):
    def body(i, carry):
        at = pl.multiple_of(start + i * 16, 16)
        for u in range(16):
            staged[pl.ds(at + u, 1), :] = source[pl.ds(index[i * 16 + u], 1), :]
        return carry

    lax.fori_loop(0, count // 16, body, 0)


def edge_forward(sel, window):
    half = dot(sel, window, 0, 0)
    up = 1.0 + jnp.tanh(half)
    act = half * up
    slope = (up + act * (2.0 - up)).astype(BF)
    total = act[0:BLK]
    for k in range(1, 8):
        total = total + act[k * BLK : (k + 1) * BLK]
    return total, slope


def edge_backward(sel, slope, half_grad):
    grad = jnp.concatenate([half_grad] * 8, axis=0) * slope
    return dot(sel, grad)


def kernel(
    n_grp, n_sub,
    h, g, wfs, wfo, wfn, wcs, wco, wcn, wpr, nbr, msk, cnbr, cmsk,
    slo_s, shi_s, cslo_s, cshi_s, slo_v, shi_v, cslo_v, cshi_v, owner,
    result, grad_h, grad_w,
    stage, halo_in, halo, far, farh, own, cidx, sel, slope, st, summed, upd, gw, acc,
    hist, hist_in, rcnt, gsend, grs, gall, tsend, trs, cin, cinf, cstaged, cstage, chalo_in, chalo, cown, cfar, cfarh,
    ccidx, csel, yc, dsc, csum, cdown, cdfar, chacc, cback, cback_in, cout, cprol, mm, dsum, down, dfar, hacc, back, back_in,
    w_e, rs_e, ge_in, all_e, w_f, rs_f, gf_in, all_f,
    halo_ss, halo_rs, hist_ss, hist_rs, grs_ss, grs_rs, gag_ss, gag_rs, trs_ss, trs_rs, tag_ss, tag_rs,
    ch_ss, ch_rs, cb_ss, cb_rs, bk_ss, bk_rs, e_ss, e_rs, eg_ss, eg_rs, ea_ss, ea_rs, f_ss, f_rs, fg_ss, fg_rs, fa_ss, fa_rs,
):
    rows = h.shape[0]
    crows = cnbr.shape[1]
    halo_rows = shi_s.shape[0]
    chalo_rows = cshi_s.shape[0]
    tiles = rows // TILE
    blocks = rows // BLK
    cblocks = crows // BLK
    hblocks = halo_rows // BLK
    quarter = crows // n_grp
    gi = lax.axis_index("grp")
    si = lax.axis_index("sub")
    above = lax.rem(si + 1, n_sub)
    below = lax.rem(si + n_sub - 1, n_sub)
    has_below = jnp.where(si > 0, 1.0, 0.0).astype(F32)
    has_above = jnp.where(si < n_sub - 1, 1.0, 0.0).astype(F32)

    def to_sub(src, dst, ss, rs, there):
        return pltpu.make_async_remote_copy(
            src_ref=src, dst_ref=dst, send_sem=ss, recv_sem=rs, device_id={"sub": there}, device_id_type=MESH
        )

    def to_grp(src, dst, ss, rs, there):
        return pltpu.make_async_remote_copy(
            src_ref=src, dst_ref=dst, send_sem=ss, recv_sem=rs, device_id={"grp": there}, device_id_type=MESH
        )

    barrier = pltpu.get_barrier_semaphore()

    def greet(d, carry):
        pl.semaphore_signal(barrier, inc=1, device_id={"sub": lax.rem(si + d, n_sub)}, device_id_type=MESH)
        return carry

    lax.fori_loop(1, n_sub, greet, 0)
    for d in range(1, n_grp):
        pl.semaphore_signal(barrier, inc=1, device_id={"grp": lax.rem(gi + d, n_grp)}, device_id_type=MESH)

    def widen(i, carry):
        upd[rows_at(i * TILE, TILE), :] = h[rows_at(i * TILE, TILE), :].astype(F32)
        return carry

    lax.fori_loop(0, tiles, widen, 0)
    gather_rows(shi_s, upd, gw, 0, halo_rows)
    gather_rows(slo_s, upd, gw, halo_rows, halo_rows)
    stage[...] = gw[0 : 2 * halo_rows, :].astype(BF)
    pl.semaphore_wait(barrier, n_sub - 1 + n_grp - 1)
    half = halo_rows // 2
    halo_copies = []
    for c in range(4):
        part = pl.ds(c * half, half)
        halo_copies.append(
            to_sub(stage.at[part], halo_in.at[part], halo_ss.at[c], halo_rs.at[c], above if c < 2 else below)
        )
        halo_copies[-1].start()

    acc[...] = jnp.zeros_like(acc)
    hist[...] = jnp.zeros_like(hist)

    def owners(i, carry):
        high, low = [], []
        for l in range(TILE // 128):
            v = owner[pl.ds(i * (TILE // 128) + l, 1), :]
            for t in range(crows // 256):
                st[i, t * 256 : (t + 1) * 256, l * 128 : (l + 1) * 128] = group_hot(v, t)
            high.append(one_hot((v >> 7).astype(F32), 16))
            low.append(one_hot((v & 127).astype(F32), 128))
        hist[...] += dot(jnp.concatenate(high, axis=1), jnp.concatenate(low, axis=1), 1, 1)
        acc[...] += dot(st[i], g[rows_at(i * TILE, TILE), :])
        return carry

    lax.fori_loop(0, tiles, owners, 0)
    hist_copies = []
    for d in range(1, n_grp):
        hist_copies.append(
            to_grp(hist, hist_in.at[d - 1], hist_ss.at[d - 1], hist_rs.at[d - 1], lax.rem(gi + d, n_grp))
        )
        hist_copies[-1].start()

    def scatter_sum(sums, send, received, ss, rs):
        copies = []
        send[...] = sums[...].astype(BF)
        for d in range(1, n_grp):
            there = lax.rem(gi + d, n_grp)
            copies.append(
                to_grp(send.at[rows_at(there * quarter, quarter)], received.at[d - 1], ss.at[d - 1], rs.at[d - 1], there)
            )
            copies[-1].start()
        return copies

    def gather_all(array, ss, rs):
        copies = []
        mine = rows_at(gi * quarter, quarter)
        for d in range(1, n_grp):
            copies.append(
                to_grp(array.at[mine], array.at[mine], ss.at[d - 1], rs.at[d - 1], lax.rem(gi + d, n_grp))
            )
            copies[-1].start()
        return copies

    def my_sum(sums, received, copies):
        for c in copies:
            c.wait_recv()
        total = sums[rows_at(gi * quarter, quarter), :]
        for d in range(1, n_grp):
            total = total + received[d - 1].astype(F32)
        return total

    grs_copies = scatter_sum(acc, gsend, grs, grs_ss, grs_rs)

    prepare_slots(nbr, msk, cidx, rows, halo_rows, hblocks)
    prepare_slots(cnbr, cmsk, ccidx, crows, chalo_rows, 1)
    both_f = jnp.concatenate([wfs[...] * 0.5, wfo[...] * 0.5], axis=1)

    def dense(i, carry):
        part = rows_at(i * TILE, TILE)
        r = dot(h[part, :], both_f)
        own[part, :] = r[:, :D].astype(BF)
        far[part, :] = r[:, D:].astype(BF)
        gw[part, :] = dot(g[part, :], wfn[...], 1, 1) * 0.5
        return carry

    lax.fori_loop(0, tiles, dense, 0)
    build_selectors(cidx, sel, blocks)

    for c in hist_copies:
        c.wait_recv()
    counts = hist[...]
    for d in range(1, n_grp):
        counts = counts + hist_in[d - 1]
    for k in range(crows // 128):
        rcnt[k * 128 : (k + 1) * 128, :] = 1.0 / jnp.maximum(
            jnp.transpose(jnp.broadcast_to(counts[k : k + 1], (128, 128))), 1.0
        )
    gall[rows_at(gi * quarter, quarter), :] = my_sum(acc, grs, grs_copies).astype(BF)
    gag_copies = gather_all(gall, gag_ss, gag_rs)
    build_selectors(ccidx, csel, cblocks)

    for c in halo_copies:
        c.wait_recv()
    halo[0:halo_rows, :] = (halo_in[0:halo_rows, :].astype(F32) * has_below).astype(BF)
    halo[halo_rows:, :] = (halo_in[halo_rows:, :].astype(F32) * has_above).astype(BF)
    farh[...] = dot(halo[...], wfo[...] * 0.5).astype(BF)

    acc[...] = jnp.zeros_like(acc)

    def forward_tile(i, carry):
        def pair(p, carry):
            for u in range(2):
                b = i * (TILE // BLK) + p * 2 + u
                hb = b & (hblocks - 1)
                window = jnp.concatenate(
                    [
                        far[rows_at(b * BLK, BLK), :],
                        farh[rows_at(hb * BLK, BLK), :],
                        farh[rows_at(halo_rows + hb * BLK, BLK), :],
                        own[rows_at(b * BLK, BLK), :],
                    ],
                    axis=0,
                )
                total, q = edge_forward(sel[b], window)
                slope[b] = q
                summed[rows_at(b * BLK, BLK), :] = total.astype(BF)
            return carry

        lax.fori_loop(0, TILE // BLK // 2, pair, 0)
        part = rows_at(i * TILE, TILE)
        new = h[part, :].astype(F32) + dot(summed[part, :], wfn[...])
        upd[part, :] = new
        acc[...] += dot(st[i], new.astype(BF))
        return carry

    lax.fori_loop(0, tiles, forward_tile, 0)

    trs_copies = scatter_sum(acc, tsend, trs, trs_ss, trs_rs)
    for c in gag_copies:
        c.wait_recv()
    yc[...] = dot(gall[...], wpr[...], 1, 1)
    dsc[...] = (dot(yc[...].astype(BF), wcn[...], 1, 1) * 0.5).astype(BF)
    mine = rows_at(gi * quarter, quarter)
    cin[mine, :] = (my_sum(acc, trs, trs_copies) * rcnt[mine, :]).astype(BF)
    tag_copies = gather_all(cin, tag_ss, tag_rs)
    for c in tag_copies:
        c.wait_recv()

    cinf[...] = cin[...].astype(F32)
    gather_rows(cshi_s, cinf, cstaged, 0, chalo_rows)
    gather_rows(cslo_s, cinf, cstaged, chalo_rows, chalo_rows)
    cstage[...] = cstaged[...].astype(BF)
    ch_copies = []
    for c in range(2):
        part = pl.ds(c * chalo_rows, chalo_rows)
        ch_copies.append(to_sub(cstage.at[part], chalo_in.at[part], ch_ss.at[c], ch_rs.at[c], (above, below)[c]))
        ch_copies[-1].start()
    r = dot(cin[...], jnp.concatenate([wcs[...] * 0.5, wco[...] * 0.5], axis=1))
    cown[...] = r[:, :D].astype(BF)
    cfar[...] = r[:, D:].astype(BF)
    for c in ch_copies:
        c.wait_recv()
    chalo[0:chalo_rows, :] = (chalo_in[0:chalo_rows, :].astype(F32) * has_below).astype(BF)
    chalo[chalo_rows:, :] = (chalo_in[chalo_rows:, :].astype(F32) * has_above).astype(BF)
    cfarh[...] = dot(chalo[...], wco[...] * 0.5).astype(BF)
    chacc[...] = jnp.zeros_like(chacc)

    def mid_pair(p, carry):
        for u in range(2):
            b = p * 2 + u
            part = rows_at(b * BLK, BLK)
            total, q = edge_forward(csel[b], jnp.concatenate([cfar[part, :], cfarh[...], cown[part, :]], axis=0))
            csum[part, :] = total.astype(BF)
            grads = edge_backward(csel[b], q, dsc[part, :])
            cdfar[part, :] = grads[0:BLK]
            chacc[...] += grads[BLK : 3 * BLK]
            cdown[part, :] = grads[3 * BLK :].astype(BF)
        return carry

    lax.fori_loop(0, cblocks // 2, mid_pair, 0)
    cback[...] = chacc[...].astype(BF)
    cb_copies = []
    for c in range(2):
        part = pl.ds(c * chalo_rows, chalo_rows)
        cb_copies.append(to_sub(cback.at[part], cback_in.at[part], cb_ss.at[c], cb_rs.at[c], (below, above)[c]))
        cb_copies[-1].start()

    cout[...] = (cin[...].astype(F32) + dot(csum[...], wcn[...])).astype(BF)
    cprol[...] = dot(cout[...], wpr[...]).astype(BF)
    shared = 1.0 / n_grp
    w_e[128:256, :] = dot(cin[...], cdown[...], 0, 0) * shared
    w_e[256:384, :] = (dot(cin[...], cdfar[...].astype(BF), 0, 0) + dot(chalo[...], cback[...], 0, 0)) * shared
    w_e[384:512, :] = dot(csum[...], yc[...].astype(BF), 0, 0) * shared
    w_e[512:640, :] = dot(cout[...], gall[...], 0, 0) * shared
    w_e[640:768, :] = jnp.zeros((128, 128), F32)

    def prolonged(i, carry):
        part = rows_at(i * TILE, TILE)
        result[part, :] = (upd[part, :] + dot(st[i], cprol[...], 0, 0)).astype(BF)
        return carry

    lax.fori_loop(0, tiles, prolonged, 0)
    for c in cb_copies:
        c.wait_recv()
    from_above = (cback_in[0:chalo_rows, :].astype(F32) * has_above).astype(BF)
    from_below = (cback_in[chalo_rows:, :].astype(F32) * has_below).astype(BF)
    for t in range(crows // 256):
        part = slice(t * 256, (t + 1) * 256)
        cdfar[part, :] += dot(group_hot(cshi_v[...], t), from_above) + dot(group_hot(cslo_v[...], t), from_below)
    dcin = yc[...] + dot(cdown[...], wcs[...], 1, 1) + dot(cdfar[...].astype(BF), wco[...], 1, 1)
    m = (dcin * rcnt[...]).astype(BF)
    mm[:, :D] = m
    mm[:, D:] = (dot(m, wfn[...], 1, 1) * 0.5).astype(BF)

    w_e[0:128, :] = jnp.zeros((128, 128), F32)

    def cotangents(i, carry):
        part = rows_at(i * TILE, TILE)
        r = dot(st[i], mm[...], 0, 0)
        y = g[part, :].astype(F32) + r[:, :D]
        upd[part, :] = y
        dsum[part, :] = (gw[part, :] + r[:, D:]).astype(BF)
        w_e[0:128, :] += dot(summed[part, :], y.astype(BF), 0, 0)
        return carry

    lax.fori_loop(0, tiles, cotangents, 0)

    def weights_scatter(array, received, ss, rs):
        size = array.shape[0] // n_sub

        def body(d, carry):
            there = lax.rem(si + d, n_sub)
            to_sub(array.at[rows_at(there * size, size)], received.at[rows_at((d - 1) * size, size)], ss, rs, there).start()
            return carry

        lax.fori_loop(1, n_sub, body, 0)

    def weights_group(array, received, group_in, ss, rs, gss, grs_):
        size = array.shape[0] // n_sub
        to_sub(received, received, ss, rs, above).wait_recv()

        def body(d, total):
            return total + received[rows_at((d - 1) * size, size), :]

        group_in[gi] = lax.fori_loop(1, n_sub, body, array[rows_at(si * size, size), :])
        copies = []
        for d in range(1, n_grp):
            copies.append(to_grp(group_in.at[gi], group_in.at[gi], gss.at[d - 1], grs_.at[d - 1], lax.rem(gi + d, n_grp)))
            copies[-1].start()
        return copies

    def weights_gather(array, group_in, copies, ss, rs):
        size = array.shape[0] // n_sub
        for c in copies:
            c.wait_recv()
        total = group_in[0]
        for k in range(1, n_grp):
            total = total + group_in[k]
        mine = rows_at(si * size, size)
        array[mine, :] = total

        def body(d, carry):
            to_sub(array.at[mine], array.at[mine], ss, rs, lax.rem(si + d, n_sub)).start()
            return carry

        lax.fori_loop(1, n_sub, body, 0)

    weights_scatter(w_e, rs_e, e_ss, e_rs)

    bk_copies = []
    for c in range(2 * hblocks):
        part = pl.ds(c * BLK, BLK)
        bk_copies.append(
            to_sub(back.at[part], back_in.at[part], bk_ss.at[c], bk_rs.at[c], below if c < hblocks else above)
        )

    def backward_halo_block(hb, carry):
        hacc[...] = jnp.zeros_like(hacc)

        def pair(p, carry):
            both = None
            for u in range(2):
                b = (p * 2 + u) * hblocks + hb
                part = rows_at(b * BLK, BLK)
                grads = edge_backward(sel[b], slope[b], dsum[part, :])
                dfar[part, :] = grads[0:BLK].astype(BF)
                down[part, :] = grads[3 * BLK :].astype(BF)
                both = grads[BLK : 3 * BLK] if both is None else both + grads[BLK : 3 * BLK]
            hacc[...] += both
            return carry

        lax.fori_loop(0, blocks // hblocks // 2, pair, 0)
        back[rows_at(hb * BLK, BLK), :] = hacc[0:BLK, :].astype(BF)
        back[rows_at(halo_rows + hb * BLK, BLK), :] = hacc[BLK:, :].astype(BF)
        for c, there in ((hb, below), (hblocks + hb, above)):
            part = rows_at(c * BLK, BLK)
            to_sub(back.at[part], back_in.at[part], bk_ss.at[c], bk_rs.at[c], there).start()
        return carry

    lax.fori_loop(0, hblocks // 2, backward_halo_block, 0)
    eg_copies = weights_group(w_e, rs_e, ge_in, e_ss, e_rs, eg_ss, eg_rs)
    lax.fori_loop(hblocks // 2, hblocks, backward_halo_block, 0)
    weights_gather(all_e, ge_in, eg_copies, ea_ss, ea_rs)

    w_f[0:128, :] = jnp.zeros((128, 128), F32)
    w_f[128:256, :] = dot(halo[...], back[...], 0, 0)

    def last_weights(i, carry):
        part = rows_at(i * TILE, TILE)
        r = dot(h[part, :], jnp.concatenate([down[part, :], dfar[part, :]], axis=1), 0, 0)
        w_f[0:128, :] += r[:, :D]
        w_f[128:256, :] += r[:, D:]
        return carry

    lax.fori_loop(0, tiles, last_weights, 0)
    weights_scatter(w_f, rs_f, f_ss, f_rs)

    def latent_part(i, carry):
        part = rows_at(i * TILE, TILE)
        upd[part, :] += dot(down[part, :], wfs[...], 1, 1) + dot(dfar[part, :], wfo[...], 1, 1)
        return carry

    lax.fori_loop(0, tiles, latent_part, 0)
    fg_copies = weights_group(w_f, rs_f, gf_in, f_ss, f_rs, fg_ss, fg_rs)

    for c in bk_copies:
        c.wait_recv()
    halo[0:halo_rows, :] = (dot(back_in[0:halo_rows, :], wfo[...], 1, 1) * has_above).astype(BF)
    halo[halo_rows:, :] = (dot(back_in[halo_rows:, :], wfo[...], 1, 1) * has_below).astype(BF)
    group = 1024

    def returned(i, carry):
        part = rows_at(i * group, group)
        hots = []
        for t in range(group // 256):
            row = []
            for table in (shi_v, slo_v):
                for l in range(halo_rows // 128):
                    row.append(group_hot(table[l : l + 1, :], i * (group // 256) + t))
            hots.append(jnp.concatenate(row, axis=1))
        grad_h[part, :] = (upd[part, :] + dot(jnp.concatenate(hots, axis=0), halo[...])).astype(BF)
        return carry

    lax.fori_loop(0, rows // group // 2, returned, 0)
    weights_gather(all_f, gf_in, fg_copies, fa_ss, fa_rs)
    lax.fori_loop(rows // group // 2, rows // group, returned, 0)

    def finish(array, ss, rs, first, count):
        size = array.shape[0] // n_sub
        others = array.at[pl.ds(0, array.shape[0] - size)]
        to_sub(others, others, ss, rs, above).wait_recv()
        for k in range(count):
            grad_w[first + k] = array[k * 128 : (k + 1) * 128, :]

    finish(all_e, ea_ss, ea_rs, 2, 5)
    finish(all_f, fa_ss, fa_rs, 0, 2)

    for c in halo_copies + hist_copies + grs_copies + gag_copies + trs_copies + tag_copies + ch_copies + cb_copies:
        c.wait_send()
    for c in bk_copies + eg_copies + fg_copies:
        c.wait_send()
    for received, array, ss, gather_ss, rs in ((rs_e, all_e, e_ss, ea_ss, e_rs), (rs_f, all_f, f_ss, fa_ss, f_rs)):
        to_sub(received, received, ss, rs, above).wait_send()
        others = array.at[pl.ds(0, array.shape[0] - array.shape[0] // n_sub)]
        to_sub(others, others, gather_ss, rs, above).wait_send()


def step(
    n_grp, n_sub,
    states, cotangent, fine_self, fine_other, fine_node, coarse_self, coarse_other, coarse_node, prolong,
    fine_nbr, fine_mask, fine_send_lo, fine_send_hi, coarse_nbr, coarse_mask, coarse_send_lo, coarse_send_hi, coarse_owner,
):
    rows, slots = fine_nbr.shape
    crows = coarse_nbr.shape[0]
    halo = fine_send_lo.shape[0]
    chalo = coarse_send_lo.shape[0]
    blocks, cblocks = rows // BLK, crows // BLK
    edges = BLK * slots
    quarter = crows // n_grp
    vmem = pl.BlockSpec(memory_space=pltpu.VMEM)
    smem = pl.BlockSpec(memory_space=pltpu.SMEM)
    V = pltpu.VMEM
    dma = pltpu.SemaphoreType.DMA
    e_rows, f_rows = 768, 256
    ce, cf = e_rows // n_sub, f_rows // n_sub
    scratch = [
        V((2 * halo, D), BF), V((2 * halo, D), BF), V((2 * halo, D), BF),
        V((rows, D), BF), V((2 * halo, D), BF), V((rows, D), BF),
        V((blocks, 8, 128), F32), V((blocks, 4 * BLK, edges), BF), V((blocks, edges, D), BF),
        V((rows // TILE, crows, TILE), BF),
        V((rows, D), BF), V((rows, D), F32), V((rows, D), F32), V((crows, D), F32),
        V((16, 128), F32), V((n_grp - 1, 16, 128), F32), V((crows, D), F32),
        V((crows, D), BF), V((n_grp - 1, quarter, D), BF), V((crows, D), BF),
        V((crows, D), BF), V((n_grp - 1, quarter, D), BF), V((crows, D), BF),
        V((crows, D), F32), V((2 * chalo, D), F32), V((2 * chalo, D), BF), V((2 * chalo, D), BF), V((2 * chalo, D), BF),
        V((crows, D), BF), V((crows, D), BF), V((2 * chalo, D), BF),
        V((cblocks, 8, 128), F32), V((cblocks, 4 * BLK, edges), BF),
        V((crows, D), F32), V((crows, D), BF), V((crows, D), BF), V((crows, D), BF), V((crows, D), F32),
        V((2 * chalo, D), F32), V((2 * chalo, D), BF), V((2 * chalo, D), BF),
        V((crows, D), BF), V((crows, D), BF), V((crows, 2 * D), BF),
        V((rows, D), BF), V((rows, D), BF), V((rows, D), BF),
        V((2 * BLK, D), F32), V((2 * halo, D), BF), V((2 * halo, D), BF),
        V((e_rows, D), F32), V((e_rows - ce, D), F32), V((n_grp, ce, D), F32), V((e_rows, D), F32),
        V((f_rows, D), F32), V((f_rows - cf, D), F32), V((n_grp, cf, D), F32), V((f_rows, D), F32),
        dma((4,)), dma((4,)),
        dma((n_grp - 1,)), dma((n_grp - 1,)), dma((n_grp - 1,)), dma((n_grp - 1,)), dma((n_grp - 1,)), dma((n_grp - 1,)),
        dma((n_grp - 1,)), dma((n_grp - 1,)), dma((n_grp - 1,)), dma((n_grp - 1,)),
        dma((2,)), dma((2,)), dma((2,)), dma((2,)),
        dma((2 * halo // BLK,)), dma((2 * halo // BLK,)),
        dma, dma, dma((n_grp - 1,)), dma((n_grp - 1,)), dma, dma,
        dma, dma, dma((n_grp - 1,)), dma((n_grp - 1,)), dma, dma,
    ]
    return pl.pallas_call(
        functools.partial(kernel, n_grp, n_sub),
        out_shape=(
            jax.ShapeDtypeStruct((rows, D), BF),
            jax.ShapeDtypeStruct((rows, D), BF),
            jax.ShapeDtypeStruct((7, D, D), F32),
        ),
        in_specs=[vmem] * 13 + [smem] * 4 + [vmem] * 5,
        out_specs=(vmem, vmem, vmem),
        scratch_shapes=scratch,
        compiler_params=pltpu.CompilerParams(
            collective_id=0, has_side_effects=True, vmem_limit_bytes=63 * 1024 * 1024
        ),
    )(
        states, cotangent, fine_self, fine_other, fine_node, coarse_self, coarse_other, coarse_node, prolong,
        fine_nbr.T, fine_mask.T, coarse_nbr.T, coarse_mask.T,
        fine_send_lo, fine_send_hi, coarse_send_lo, coarse_send_hi,
        fine_send_lo.reshape(-1, 128), fine_send_hi.reshape(-1, 128),
        coarse_send_lo.reshape(1, -1), coarse_send_hi.reshape(1, -1),
        coarse_owner.reshape(-1, 128),
    )


def solution(mesh):
    rows2 = P(("grp", "sub"), None)
    rows1 = P(("grp", "sub"))
    in_specs = (
        (rows2, rows2) + (P(),) * 7
        + (rows2, rows2, rows1, rows1)
        + (P("sub", None), P("sub", None), P("sub"), P("sub"), rows1)
    )
    return jax.shard_map(
        functools.partial(step, mesh.shape["grp"], mesh.shape["sub"]),
        mesh=mesh, in_specs=in_specs, out_specs=(rows2, rows2, P()), check_vma=False,
    )
```

time: 555 us -> 112 us (0.20); the launches traced: 545 us -> 111 us
  waiting for transfers between devices: 158 us -> 0 us
  matrix products: 149 us -> 0 us
  Pallas kernels: 0 us -> 106 us
  other arithmetic: 96.8 us -> 0 us
  local copies, waits for them, and re-layouts: 78.2 us -> 4.45 us
  starting transfers between devices: 40.7 us -> 0 us
  between operations: 14.8 us -> 0.66 us
  blocking collectives: 6.36 us -> 0 us
    psum x3 -> x0, waiting for transfers between devices: 157 us -> none  [the longest x1 153 us: per_device(): lax.psum(jnp.stack([grad_fself, grad_fother, grad_fnode, 0.25 * grad_csel...]
    dot_general x35 -> x0, matrix products: 149 us -> none  [the longest x5 38.2 us: advance(): jnp.einsum('grc,gcd->grd', selector, window_block, preferred_element_type...]
    pallas_call x0 -> x1, Pallas kernels: none -> 106 us  [step(): pl.pallas_call(functools.partial(kernel, n_grp, n_sub), out_shape=(jax.Sh...]
    scatter-add x3 -> x0, other arithmetic: 74.7 us -> none  [the longest x1 28.8 us: per_device(): jax.ops.segment_sum(jnp.ones(coarse_owner.shape[0], jnp.float32), coarse_...]
    ppermute x8 -> x0, starting transfers between devices: 40.6 us -> none  [shifted(): return lax.ppermute(block, axis, route)]
    gather x6 -> x0, local copies, waits for them, and re-layouts: 27.7 us -> none  [the longest x1 12.1 us: per_device(): picked = coarse_out[coarse_owner]]
    add x8 -> x0, local copies, waits for them, and re-layouts: 12.7 us -> none  [advance(): preact = own_block[:, :, None, :] + picked]
    add x2 -> x0, other arithmetic: 11.5 us -> none  [level_backward(): grad_local + jax.ops.segment_sum(back_up, send_lo, num_segments=rows)]
  transfers between devices with their start and end apart: 11 -> 0, of which waited for: 4 -> 0; matrix products, arithmetic and copies ran while one was open for 27% -> 0% of each run, Pallas kernels for 0% -> 0%
where the time goes in v1:
time: 112 us; the launch traced here: 111 us
  Pallas kernels  106 us (95%)
  local copies, waits for them, and re-layouts  4.45 us (4%)
    pallas_call x1, Pallas kernels, step(): pl.pallas_call(functools.partial(kernel, n_grp, n_sub), out_shape=(jax.Sh...  106 us
    unnamed x7, local copies, waits for them, and re-layouts  4.45 us

profile of v1, /device:TPU:1, one launch (start us, length us, event | category | flops | bytes accessed | tf_op | source)
XLA Modules:
  0.0 111.2 jit_solution(6296441868385172286)
XLA Ops:
  0.6 106.1 %shard_map.193 = (bf16[4096,128]{1,0:T(8,128)(2,1)}, bf16[4096,128]{1,0:T(8,128)(2,1)}, f32[7,128,128]{2,1,0:T(8,128)}) custom-call(bf16[4096,128]{1,0:T(8,128)(2,1)} %h.1, bf16[4096,128]{1,0:T(8,128)(2,1)} %g.1, bf16[128,128]{1,0:T(8,128)(2,1)} %wfs.1, bf16[128,128]{1,0:T(8,128)(2,1)} %wfo.1, bf16[128,128]{1,0:T(8,128)(2,1)} %wfn.1, bf16[128,128]{1,0:T(8,128)(2,1)} %wcs.1, ...), custom_call_target="tpu_custom_call" | custom-call | tf_op jit(solution)/shard_map/pallas_call | solution.py:572
  106.7 0.0 copy-start
  106.8 2.4 %copy.24 = bf16[4096,128]{1,0:T(8,128)(2,1)} copy(bf16[4096,128]{1,0:T(8,128)(2,1)} %get-tuple-element.6) | data formatting | bytes 2097152
  109.1 0.0 copy-done
  109.1 0.0 copy-start.1
  109.1 1.0 copy.25
  110.1 0.4 copy-done.1
  110.4 0.8 copy.26
Async XLA Ops:
  106.7 2.4 %copy-start = (bf16[4096,128]{1,0:T(8,128)(2,1)S(1)}, bf16[4096,128]{1,0:T(8,128)(2,1)}, u32[]{:S(2)}) copy-start(bf16[4096,128]{1,0:T(8,128)(2,1)} %get-tuple-element.7) | copy-start | bytes 3145732
  109.1 1.3 %copy-start.1 = (f32[7,128,128]{2,1,0:T(8,128)S(1)}, f32[7,128,128]{2,1,0:T(8,128)}, u32[]{:S(2)}) copy-start(f32[7,128,128]{2,1,0:T(8,128)} %get-tuple-element.8) | copy-start | bytes 1376260

commit v2 on v1

v2 whole, which is shorter than its diff:
```python
import functools

import jax
import jax.numpy as jnp
from jax import lax
from jax.experimental import pallas as pl
from jax.experimental.pallas import tpu as pltpu
from jax.sharding import PartitionSpec as P

MESH = pl.DeviceIdType.MESH
BF = jnp.bfloat16
F32 = jnp.float32
D = 128
BLK = 64
TILE = 512


def dot(a, b, ca=1, cb=0):
    return lax.dot_general(a, b, (((ca,), (cb,)), ((), ())), preferred_element_type=F32)


def rows_at(start, size):
    if isinstance(start, int):
        return pl.ds(start, size)
    return pl.ds(pl.multiple_of(start, size if size % 8 == 0 else 8), size)


def spread(row, rows):
    one = jnp.broadcast_to(row, (16, row.shape[1])).astype(BF)
    return jnp.concatenate([one] * (rows // 16), axis=0)


def iota_bf(rows, lanes, base=0):
    return (lax.broadcasted_iota(jnp.int32, (rows, lanes), 0) + base).astype(F32).astype(BF)


def one_hot(row, rows, base=0):
    hit = iota_bf(rows, row.shape[1], base) == spread(row, rows)
    return jnp.where(hit, jnp.ones((), BF), jnp.zeros((), BF))


def group_hot(values, group):
    inside = jnp.where((values >> 8) == group, values & 255, -1).astype(F32)
    return one_hot(inside, 256)


def prepare_slots(nbr, msk, cidx, rows, halo, halo_blocks):
    def body(p, carry):
        v = nbr[:, rows_at(p * 128, 128)]
        used = msk[:, rows_at(p * 128, 128)] > 0
        lane = lax.broadcasted_iota(jnp.int32, (8, 128), 1)
        slot = lax.broadcasted_iota(jnp.int32, (8, 128), 0)
        blk = 2 * p + (lane >> 6)
        hblk = blk & (halo_blocks - 1)
        col = jnp.where(
            v < rows,
            v - blk * BLK,
            jnp.where(v < rows + halo, v - rows - hblk * BLK + BLK, v - rows - halo - hblk * BLK + 2 * BLK),
        )
        col = jnp.where(used, col, -1)
        own = jnp.where(used, 3 * BLK + (lane & (BLK - 1)), -1)
        first = lane < BLK

        def halves(x):
            later = pltpu.roll(x, 4, 0)
            return (
                jnp.where(first, x, pltpu.roll(later, BLK, 1)),
                jnp.where(first, pltpu.roll(x, BLK, 1), later),
            )

        for half, (c, o) in enumerate(zip(halves(col), halves(own))):
            cidx[2 * p + half] = jnp.where(slot < 4, c, pltpu.roll(o, 4, 0)).astype(F32)
        return carry

    lax.fori_loop(0, rows // 128, body, 0)


def build_selectors(cidx, sel, blocks):
    def body(p, carry):
        for u in range(4):
            b = p * 4 + u
            idx = cidx[b]
            for j in range(4):
                sel[b, 0 : 3 * BLK, j * 128 : (j + 1) * 128] = one_hot(idx[j : j + 1], 3 * BLK)
                sel[b, 3 * BLK : 4 * BLK, j * 128 : (j + 1) * 128] = one_hot(idx[4 + j : 5 + j], BLK, 3 * BLK)
        return carry

    lax.fori_loop(0, blocks // 4, body, 0)


def gather_rows(index, source, staged, start, count):
    def body(i, carry):
        at = pl.multiple_of(start + i * 16, 16)
        for u in range(16):
            staged[pl.ds(at + u, 1), :] = source[pl.ds(index[i * 16 + u], 1), :]
        return carry

    lax.fori_loop(0, count // 16, body, 0)


def edge_forward(sel, window):
    half = dot(sel, window, 0, 0)
    up = 1.0 + jnp.tanh(half)
    act = half * up
    slope = (up + act * (2.0 - up)).astype(BF)
    total = act[0:BLK]
    for k in range(1, 8):
        total = total + act[k * BLK : (k + 1) * BLK]
    return total, slope


def edge_backward(sel, slope, half_grad):
    grad = jnp.concatenate([half_grad] * 8, axis=0) * slope
    return dot(sel, grad)


def kernel(
    n_grp, n_sub,
    h_hbm, g_hbm, wfs, wfo, wfn, wcs, wco, wcn, wpr, nbr_hbm, msk_hbm, cnbr_hbm, cmsk_hbm,
    slo_s, shi_s, cslo_s, cshi_s, slo_v, shi_v, cslo_v, cshi_v, owner,
    result_hbm, grad_h_hbm, grad_w,
    h, g, nbr, msk, cnbr, cmsk, result, grad_h,
    stage, halo_in, halo, far_dfar, farh, own_dsum, cidx, sel, slope, st, summed_down, upd, rowbuf, acc,
    hist, hist_in, rcnt, gsend, gcore, gchip, gx, gall, tsend, tcore, tchip, tx, cin, cinf, cstaged, cstage, chalo_in, chalo, cown, cfar, cfarh,
    ccidx, csel, yc, dsc, csum, cdown, cdfar, chacc, cback, cback_in, cout, cprol, mm, back, back_in,
    w_e, rs_e, all_e, w_f, sum_f, rs_f, grp_f, all_f,
    load_s, store_s, halo_ss, halo_rs, hist_ss, hist_rs, gs_ss, gs_rs, ts_ss, ts_rs,
    ch_ss, ch_rs, cb_ss, cb_rs, bk_ss, bk_rs, e_ss, e_rs, ea_ss, ea_rs, f_ss, f_rs, fg_ss, fg_rs, fa_ss, fa_rs,
):
    own, dsum = own_dsum, own_dsum
    far, dfar = far_dfar, far_dfar
    summed, down = summed_down, summed_down
    gw = rowbuf
    rows = h.shape[0]
    crows = cnbr.shape[1]
    halo_rows = shi_s.shape[0]
    chalo_rows = cshi_s.shape[0]
    tiles = rows // TILE
    blocks = rows // BLK
    cblocks = crows // BLK
    hblocks = halo_rows // BLK
    gi = lax.axis_index("grp")
    si = lax.axis_index("sub")
    above = lax.rem(si + 1, n_sub)
    below = lax.rem(si + n_sub - 1, n_sub)
    has_below = jnp.where(si > 0, 1.0, 0.0).astype(F32)
    has_above = jnp.where(si < n_sub - 1, 1.0, 0.0).astype(F32)

    def to_sub(src, dst, ss, rs, there):
        return pltpu.make_async_remote_copy(
            src_ref=src, dst_ref=dst, send_sem=ss, recv_sem=rs, device_id={"sub": there}, device_id_type=MESH
        )

    def to_grp(src, dst, ss, rs, there):
        return pltpu.make_async_remote_copy(
            src_ref=src, dst_ref=dst, send_sem=ss, recv_sem=rs, device_id={"grp": there}, device_id_type=MESH
        )

    loads = []
    for k, (src, dst) in enumerate(
        ((h_hbm, h), (g_hbm, g), (nbr_hbm, nbr), (msk_hbm, msk), (cnbr_hbm, cnbr), (cmsk_hbm, cmsk))
    ):
        loads.append(pltpu.make_async_copy(src, dst, load_s.at[k]))
        loads[-1].start()

    def weights_scatter(array, received, ss, rs):
        size = array.shape[0] // n_sub

        def body(d, carry):
            there = lax.rem(si + d, n_sub)
            to_sub(array.at[rows_at(there * size, size)], received.at[rows_at((d - 1) * size, size)], ss, rs, there).start()
            return carry

        lax.fori_loop(1, n_sub, body, 0)

    def weights_sum(array, received, ss, rs):
        size = array.shape[0] // n_sub
        to_sub(received, received, ss, rs, above).wait_recv()

        def body(d, total):
            return total + received[rows_at((d - 1) * size, size), :].astype(F32)

        return lax.fori_loop(1, n_sub, body, array[rows_at(si * size, size), :].astype(F32))

    def weights_gather(array, total, ss, rs):
        size = array.shape[0] // n_sub
        mine = rows_at(si * size, size)
        array[mine, :] = total.astype(BF)

        def body(d, carry):
            to_sub(array.at[mine], array.at[mine], ss, rs, lax.rem(si + d, n_sub)).start()
            return carry

        lax.fori_loop(1, n_sub, body, 0)

    barrier = pltpu.get_barrier_semaphore()

    def greet(d, carry):
        pl.semaphore_signal(barrier, inc=1, device_id={"sub": lax.rem(si + d, n_sub)}, device_id_type=MESH)
        return carry

    lax.fori_loop(1, n_sub, greet, 0)
    for d in range(1, n_grp):
        pl.semaphore_signal(barrier, inc=1, device_id={"grp": lax.rem(gi + d, n_grp)}, device_id_type=MESH)

    def widen(i, carry):
        upd[rows_at(i * TILE, TILE), :] = h[rows_at(i * TILE, TILE), :].astype(F32)
        return carry

    loads[0].wait()
    lax.fori_loop(0, tiles, widen, 0)
    gather_rows(shi_s, upd, rowbuf, 0, halo_rows)
    gather_rows(slo_s, upd, rowbuf, halo_rows, halo_rows)
    stage[...] = rowbuf[0 : 2 * halo_rows, :].astype(BF)
    pl.semaphore_wait(barrier, n_sub - 1 + n_grp - 1)
    half = halo_rows // 2
    halo_copies = []
    for c in range(4):
        part = pl.ds(c * half, half)
        halo_copies.append(
            to_sub(stage.at[part], halo_in.at[part], halo_ss.at[c], halo_rs.at[c], above if c < 2 else below)
        )
        halo_copies[-1].start()

    loads[1].wait()
    acc[...] = jnp.zeros_like(acc)
    hist[...] = jnp.zeros_like(hist)

    def owners(i, carry):
        high, low = [], []
        for l in range(TILE // 128):
            v = owner[pl.ds(i * (TILE // 128) + l, 1), :]
            for t in range(crows // 256):
                st[i, t * 256 : (t + 1) * 256, l * 128 : (l + 1) * 128] = group_hot(v, t)
            high.append(one_hot((v >> 7).astype(F32), 16))
            low.append(one_hot((v & 127).astype(F32), 128))
        hist[...] += dot(jnp.concatenate(high, axis=1), jnp.concatenate(low, axis=1), 1, 1)
        acc[...] += dot(st[i], g[rows_at(i * TILE, TILE), :])
        return carry

    lax.fori_loop(0, tiles, owners, 0)
    hist_copies = []
    for d in range(1, n_grp):
        hist_copies.append(
            to_grp(hist, hist_in.at[d - 1], hist_ss.at[d - 1], hist_rs.at[d - 1], lax.rem(gi + d, n_grp))
        )
        hist_copies[-1].start()

    core = lax.rem(gi, 2)
    sibling = gi + 1 - 2 * core
    other_chip = lax.rem(gi + 2, n_grp)
    part_rows = crows // 2
    mine = rows_at(core * part_rows, part_rows)
    theirs = rows_at((1 - core) * part_rows, part_rows)

    def group_first(sums, send, received, ss, rs):
        send[...] = sums[...].astype(BF)
        copy = to_grp(send.at[theirs], received, ss.at[0], rs.at[0], sibling)
        copy.start()
        return [copy]

    def group_second(copies, sums, received, chip, other, ss, rs):
        copies[0].wait_recv()
        chip[...] = (sums[mine, :] + received[...].astype(F32)).astype(BF)
        copies.append(to_grp(chip, other, ss.at[1], rs.at[1], other_chip))
        copies[1].start()

    def group_third(copies, chip, other, scale, whole, ss, rs):
        copies[1].wait_recv()
        total = chip[...].astype(F32) + other[...].astype(F32)
        whole[mine, :] = (total if scale is None else total * scale[mine, :]).astype(BF)
        copies.append(to_grp(whole.at[mine], whole.at[mine], ss.at[2], rs.at[2], sibling))
        copies[2].start()

    g_copies = group_first(acc, gsend, gcore, gs_ss, gs_rs)

    for c in loads[2:]:
        c.wait()
    prepare_slots(nbr, msk, cidx, rows, halo_rows, hblocks)
    both_f = jnp.concatenate([wfs[...] * 0.5, wfo[...] * 0.5], axis=1)

    def dense(i, carry):
        part = rows_at(i * TILE, TILE)
        r = dot(h[part, :], both_f)
        own[part, :] = r[:, :D].astype(BF)
        far[part, :] = r[:, D:].astype(BF)
        return carry

    lax.fori_loop(0, tiles, dense, 0)
    build_selectors(cidx, sel, blocks)

    group_second(g_copies, acc, gcore, gchip, gx, gs_ss, gs_rs)

    for c in halo_copies:
        c.wait_recv()
    halo[0:halo_rows, :] = (halo_in[0:halo_rows, :].astype(F32) * has_below).astype(BF)
    halo[halo_rows:, :] = (halo_in[halo_rows:, :].astype(F32) * has_above).astype(BF)
    farh[...] = dot(halo[...], wfo[...] * 0.5).astype(BF)

    acc[...] = jnp.zeros_like(acc)

    def forward_edges(i):
        for u in range(TILE // BLK):
            b = i * (TILE // BLK) + u
            hb = b & (hblocks - 1)
            window = jnp.concatenate(
                [
                    far[rows_at(b * BLK, BLK), :],
                    farh[rows_at(hb * BLK, BLK), :],
                    farh[rows_at(halo_rows + hb * BLK, BLK), :],
                    own[rows_at(b * BLK, BLK), :],
                ],
                axis=0,
            )
            total, q = edge_forward(sel[b], window)
            slope[b] = q
            summed[rows_at(b * BLK, BLK), :] = total.astype(BF)

    def forward_update(i):
        part = rows_at(i * TILE, TILE)
        new = h[part, :].astype(F32) + dot(summed[part, :], wfn[...])
        upd[part, :] = new
        acc[...] += dot(st[i], new.astype(BF))

    def forward_tiles(p, carry):
        forward_update(p * 2 - 2)
        forward_update(p * 2 - 1)
        forward_edges(p * 2)
        forward_edges(p * 2 + 1)
        return carry

    forward_edges(0)
    forward_edges(1)
    lax.fori_loop(1, tiles // 2, forward_tiles, 0)
    forward_update(tiles - 2)
    forward_update(tiles - 1)

    group_third(g_copies, gchip, gx, None, gall, gs_ss, gs_rs)
    t_copies = group_first(acc, tsend, tcore, ts_ss, ts_rs)
    for c in hist_copies:
        c.wait_recv()
    counts = hist[...]
    for d in range(1, n_grp):
        counts = counts + hist_in[d - 1]
    for k in range(crows // 128):
        rcnt[k * 128 : (k + 1) * 128, :] = 1.0 / jnp.maximum(
            jnp.transpose(jnp.broadcast_to(counts[k : k + 1], (128, 128))), 1.0
        )
    prepare_slots(cnbr, cmsk, ccidx, crows, chalo_rows, 1)
    g_copies[2].wait_recv()
    yc[...] = dot(gall[...], wpr[...], 1, 1)
    group_second(t_copies, acc, tcore, tchip, tx, ts_ss, ts_rs)
    dsc[...] = (dot(yc[...].astype(BF), wcn[...], 1, 1) * 0.5).astype(BF)
    build_selectors(ccidx, csel, cblocks)
    group_third(t_copies, tchip, tx, rcnt, cin, ts_ss, ts_rs)
    t_copies[2].wait_recv()

    cinf[...] = cin[...].astype(F32)
    gather_rows(cshi_s, cinf, cstaged, 0, chalo_rows)
    gather_rows(cslo_s, cinf, cstaged, chalo_rows, chalo_rows)
    cstage[...] = cstaged[...].astype(BF)
    ch_copies = []
    for c in range(2):
        part = pl.ds(c * chalo_rows, chalo_rows)
        ch_copies.append(to_sub(cstage.at[part], chalo_in.at[part], ch_ss.at[c], ch_rs.at[c], (above, below)[c]))
        ch_copies[-1].start()
    r = dot(cin[...], jnp.concatenate([wcs[...] * 0.5, wco[...] * 0.5], axis=1))
    cown[...] = r[:, :D].astype(BF)
    cfar[...] = r[:, D:].astype(BF)

    def known_part(i, carry):
        part = rows_at(i * TILE, TILE)
        gw[part, :] = dot(g[part, :], wfn[...], 1, 1) * 0.5
        return carry

    lax.fori_loop(0, tiles, known_part, 0)
    for c in ch_copies:
        c.wait_recv()
    chalo[0:chalo_rows, :] = (chalo_in[0:chalo_rows, :].astype(F32) * has_below).astype(BF)
    chalo[chalo_rows:, :] = (chalo_in[chalo_rows:, :].astype(F32) * has_above).astype(BF)
    cfarh[...] = dot(chalo[...], wco[...] * 0.5).astype(BF)
    chacc[...] = jnp.zeros_like(chacc)

    def mid_blocks(p, carry):
        both = None
        for u in range(8):
            b = p * 8 + u
            part = rows_at(b * BLK, BLK)
            total, q = edge_forward(csel[b], jnp.concatenate([cfar[part, :], cfarh[...], cown[part, :]], axis=0))
            csum[part, :] = total.astype(BF)
            grads = edge_backward(csel[b], q, dsc[part, :])
            cdfar[part, :] = grads[0:BLK]
            both = grads[BLK : 3 * BLK] if both is None else both + grads[BLK : 3 * BLK]
            cdown[part, :] = grads[3 * BLK :].astype(BF)
        chacc[...] += both
        return carry

    lax.fori_loop(0, cblocks // 8, mid_blocks, 0)
    cback[...] = chacc[...].astype(BF)
    cb_copies = []
    for c in range(2):
        part = pl.ds(c * chalo_rows, chalo_rows)
        cb_copies.append(to_sub(cback.at[part], cback_in.at[part], cb_ss.at[c], cb_rs.at[c], (below, above)[c]))
        cb_copies[-1].start()

    cout[...] = (cin[...].astype(F32) + dot(csum[...], wcn[...])).astype(BF)
    cprol[...] = dot(cout[...], wpr[...]).astype(BF)
    w_e[0:128, :] = dot(cin[...], cdown[...], 0, 0).astype(BF)
    w_e[128:256, :] = (dot(cin[...], cdfar[...].astype(BF), 0, 0) + dot(chalo[...], cback[...], 0, 0)).astype(BF)
    w_e[256:384, :] = dot(csum[...], yc[...].astype(BF), 0, 0).astype(BF)
    w_e[384:512, :] = dot(cout[...], gall[...], 0, 0).astype(BF)
    weights_scatter(w_e, rs_e, e_ss, e_rs)

    def prolonged(p, carry):
        for u in range(2):
            i = p * 2 + u
            part = rows_at(i * TILE, TILE)
            result[part, :] = (upd[part, :] + dot(st[i], cprol[...], 0, 0)).astype(BF)
        return carry

    lax.fori_loop(0, tiles // 2, prolonged, 0)
    stores = [pltpu.make_async_copy(result, result_hbm, store_s.at[0])]
    stores[0].start()
    for c in cb_copies:
        c.wait_recv()
    from_above = (cback_in[0:chalo_rows, :].astype(F32) * has_above).astype(BF)
    from_below = (cback_in[chalo_rows:, :].astype(F32) * has_below).astype(BF)
    for t in range(crows // 256):
        part = slice(t * 256, (t + 1) * 256)
        cdfar[part, :] += dot(group_hot(cshi_v[...], t), from_above) + dot(group_hot(cslo_v[...], t), from_below)
    dcin = yc[...] + dot(cdown[...], wcs[...], 1, 1) + dot(cdfar[...].astype(BF), wco[...], 1, 1)
    m = (dcin * rcnt[...]).astype(BF)
    mm[:, :D] = m
    mm[:, D:] = (dot(m, wfn[...], 1, 1) * 0.5).astype(BF)
    weights_gather(all_e, weights_sum(w_e, rs_e, e_ss, e_rs), ea_ss, ea_rs)

    sum_f[...] = jnp.zeros_like(sum_f)

    def cotangents(p, carry):
        for u in range(2):
            i = p * 2 + u
            part = rows_at(i * TILE, TILE)
            r = dot(st[i], mm[...], 0, 0)
            y = g[part, :].astype(F32) + r[:, :D]
            upd[part, :] = y
            dsum[part, :] = (gw[part, :] + r[:, D:]).astype(BF)
            sum_f[256:384, :] += dot(summed[part, :], y.astype(BF), 0, 0)
        return carry

    lax.fori_loop(0, tiles // 2, cotangents, 0)

    bk_copies = []
    for c in range(2 * hblocks):
        part = pl.ds(c * BLK, BLK)
        bk_copies.append(
            to_sub(back.at[part], back_in.at[part], bk_ss.at[c], bk_rs.at[c], below if c < hblocks else above)
        )

    def backward_edges(hb):
        both = None
        for u in range(blocks // hblocks):
            b = u * hblocks + hb
            part = rows_at(b * BLK, BLK)
            grads = edge_backward(sel[b], slope[b], dsum[part, :])
            dfar[part, :] = grads[0:BLK].astype(BF)
            down[part, :] = grads[3 * BLK :].astype(BF)
            both = grads[BLK : 3 * BLK] if both is None else both + grads[BLK : 3 * BLK]
        back[rows_at(hb * BLK, BLK), :] = both[0:BLK].astype(BF)
        back[rows_at(halo_rows + hb * BLK, BLK), :] = both[BLK:].astype(BF)
        for c, there in ((hb, below), (hblocks + hb, above)):
            part = rows_at(c * BLK, BLK)
            to_sub(back.at[part], back_in.at[part], bk_ss.at[c], bk_rs.at[c], there).start()

    def backward_dense(hb):
        parts = [rows_at((u * hblocks + hb) * BLK, BLK) for u in range(blocks // hblocks)]
        grads = jnp.concatenate([jnp.concatenate([down[p, :], dfar[p, :]], axis=1) for p in parts], axis=0)
        r = dot(jnp.concatenate([h[p, :] for p in parts], axis=0), grads, 0, 0)
        sum_f[0:128, :] += r[:, :D]
        sum_f[128:256, :] += r[:, D:]
        r = dot(grads, jnp.concatenate([wfs[...], wfo[...]], axis=1), 1, 1)
        for u, p in enumerate(parts):
            upd[p, :] += r[u * BLK : (u + 1) * BLK]

    def backward_step(hb, carry):
        backward_dense(hb - 1)
        backward_edges(hb)
        return carry

    backward_edges(0)
    lax.fori_loop(1, hblocks, backward_step, 0)
    sum_f[128:256, :] += dot(halo[...], back[...], 0, 0)
    backward_dense(hblocks - 1)
    w_f[...] = sum_f[...].astype(BF)
    weights_scatter(w_f, rs_f, f_ss, f_rs)

    grp_f[gi] = weights_sum(w_f, rs_f, f_ss, f_rs)
    fg_copies = []
    for d in range(1, n_grp):
        fg_copies.append(to_grp(grp_f.at[gi], grp_f.at[gi], fg_ss.at[d - 1], fg_rs.at[d - 1], lax.rem(gi + d, n_grp)))
        fg_copies[-1].start()
    for c in bk_copies:
        c.wait_recv()
    halo[0:halo_rows, :] = (dot(back_in[0:halo_rows, :], wfo[...], 1, 1) * has_above).astype(BF)
    halo[halo_rows:, :] = (dot(back_in[halo_rows:, :], wfo[...], 1, 1) * has_below).astype(BF)
    group = 1024

    def returned(i, carry):
        part = rows_at(i * group, group)
        hots = []
        for t in range(group // 256):
            row = []
            for table in (shi_v, slo_v):
                for l in range(halo_rows // 128):
                    row.append(group_hot(table[l : l + 1, :], i * (group // 256) + t))
            hots.append(jnp.concatenate(row, axis=1))
        grad_h[part, :] = (upd[part, :] + dot(jnp.concatenate(hots, axis=0), halo[...])).astype(BF)
        return carry

    lax.fori_loop(0, rows // group // 2, returned, 0)
    for c in fg_copies:
        c.wait_recv()
    total = grp_f[0]
    for k in range(1, n_grp):
        total = total + grp_f[k]
    weights_gather(all_f, total, fa_ss, fa_rs)
    lax.fori_loop(rows // group // 2, rows // group, returned, 0)
    stores.append(pltpu.make_async_copy(grad_h, grad_h_hbm, store_s.at[1]))
    stores[1].start()

    def finish(array, ss, rs, first, count):
        size = array.shape[0] // n_sub
        others = array.at[pl.ds(0, array.shape[0] - size)]
        to_sub(others, others, ss, rs, above).wait_recv()
        for k in range(count):
            grad_w[first + k] = array[k * 128 : (k + 1) * 128, :].astype(F32)

    finish(all_e, ea_ss, ea_rs, 3, 4)
    finish(all_f, fa_ss, fa_rs, 0, 3)

    for c in halo_copies + hist_copies + g_copies + t_copies + ch_copies + cb_copies:
        c.wait_send()
    for c in bk_copies + fg_copies:
        c.wait_send()
    for c in stores:
        c.wait()
    for received, array, ss, gather_ss, rs in ((rs_e, all_e, e_ss, ea_ss, e_rs), (rs_f, all_f, f_ss, fa_ss, f_rs)):
        to_sub(received, received, ss, rs, above).wait_send()
        others = array.at[pl.ds(0, array.shape[0] - array.shape[0] // n_sub)]
        to_sub(others, others, gather_ss, rs, above).wait_send()


def step(
    n_grp, n_sub,
    states, cotangent, fine_self, fine_other, fine_node, coarse_self, coarse_other, coarse_node, prolong,
    fine_nbr, fine_mask, fine_send_lo, fine_send_hi, coarse_nbr, coarse_mask, coarse_send_lo, coarse_send_hi, coarse_owner,
):
    rows, slots = fine_nbr.shape
    crows = coarse_nbr.shape[0]
    halo = fine_send_lo.shape[0]
    chalo = coarse_send_lo.shape[0]
    blocks, cblocks = rows // BLK, crows // BLK
    edges = BLK * slots
    vmem = pl.BlockSpec(memory_space=pltpu.VMEM)
    smem = pl.BlockSpec(memory_space=pltpu.SMEM)
    hbm = pl.BlockSpec(memory_space=pl.ANY)
    V = pltpu.VMEM
    dma = pltpu.SemaphoreType.DMA
    w_rows = 4 * D
    wc = w_rows // n_sub
    i32 = jnp.int32
    scratch = [
        V((rows, D), BF), V((rows, D), BF), V((slots, rows), i32), V((slots, rows), i32),
        V((slots, crows), i32), V((slots, crows), i32), V((rows, D), BF), V((rows, D), BF),
        V((2 * halo, D), BF), V((2 * halo, D), BF), V((2 * halo, D), BF),
        V((rows, D), BF), V((2 * halo, D), BF), V((rows, D), BF),
        V((blocks, 8, 128), F32), V((blocks, 4 * BLK, edges), BF), V((blocks, edges, D), BF),
        V((rows // TILE, crows, TILE), BF),
        V((rows, D), BF), V((rows, D), F32), V((rows, D), F32), V((crows, D), F32),
        V((16, 128), F32), V((n_grp - 1, 16, 128), F32), V((crows, D), F32),
        V((crows, D), BF), V((crows // 2, D), BF), V((crows // 2, D), BF), V((crows // 2, D), BF), V((crows, D), BF),
        V((crows, D), BF), V((crows // 2, D), BF), V((crows // 2, D), BF), V((crows // 2, D), BF), V((crows, D), BF),
        V((crows, D), F32), V((2 * chalo, D), F32), V((2 * chalo, D), BF), V((2 * chalo, D), BF), V((2 * chalo, D), BF),
        V((crows, D), BF), V((crows, D), BF), V((2 * chalo, D), BF),
        V((cblocks, 8, 128), F32), V((cblocks, 4 * BLK, edges), BF),
        V((crows, D), F32), V((crows, D), BF), V((crows, D), BF), V((crows, D), BF), V((crows, D), F32),
        V((2 * chalo, D), F32), V((2 * chalo, D), BF), V((2 * chalo, D), BF),
        V((crows, D), BF), V((crows, D), BF), V((crows, 2 * D), BF),
        V((2 * halo, D), BF), V((2 * halo, D), BF),
        V((w_rows, D), BF), V((w_rows - wc, D), BF), V((w_rows, D), BF),
        V((w_rows, D), BF), V((w_rows, D), F32), V((w_rows - wc, D), BF), V((n_grp, wc, D), F32), V((w_rows, D), BF),
        dma((6,)), dma((2,)), dma((4,)), dma((4,)),
        dma((n_grp - 1,)), dma((n_grp - 1,)), dma((3,)), dma((3,)), dma((3,)), dma((3,)),
        dma((2,)), dma((2,)), dma((2,)), dma((2,)),
        dma((2 * halo // BLK,)), dma((2 * halo // BLK,)),
        dma, dma, dma, dma,
        dma, dma, dma((n_grp - 1,)), dma((n_grp - 1,)), dma, dma,
    ]
    outs = pl.pallas_call(
        functools.partial(kernel, n_grp, n_sub),
        out_shape=(
            jax.ShapeDtypeStruct((rows, D), BF),
            jax.ShapeDtypeStruct((rows, D), BF),
            jax.ShapeDtypeStruct((7, D, D), F32),
        ),
        in_specs=[hbm] * 2 + [vmem] * 7 + [hbm] * 4 + [smem] * 4 + [vmem] * 5,
        out_specs=(hbm, hbm, vmem),
        scratch_shapes=scratch,
        compiler_params=pltpu.CompilerParams(
            collective_id=0, has_side_effects=True, vmem_limit_bytes=63 * 1024 * 1024
        ),
    )(
        states, cotangent, fine_self, fine_other, fine_node, coarse_self, coarse_other, coarse_node, prolong,
        fine_nbr.T, fine_mask.T, coarse_nbr.T, coarse_mask.T,
        fine_send_lo, fine_send_hi, coarse_send_lo, coarse_send_hi,
        fine_send_lo.reshape(-1, 128), fine_send_hi.reshape(-1, 128),
        coarse_send_lo.reshape(1, -1), coarse_send_hi.reshape(1, -1),
        coarse_owner.reshape(-1, 128),
    )
    return outs


def solution(mesh):
    rows2 = P(("grp", "sub"), None)
    rows1 = P(("grp", "sub"))
    in_specs = (
        (rows2, rows2) + (P(),) * 7
        + (rows2, rows2, rows1, rows1)
        + (P("sub", None), P("sub", None), P("sub"), P("sub"), rows1)
    )
    return jax.shard_map(
        functools.partial(step, mesh.shape["grp"], mesh.shape["sub"]),
        mesh=mesh, in_specs=in_specs, out_specs=(rows2, rows2, P()), check_vma=False,
    )
```

time: 112 us -> 90.5 us (0.81)
  Pallas kernels: 106 us -> 85.1 us
    pallas_call x1, Pallas kernels: 106 us -> 85.1 us  [step(): pl.pallas_call(functools.partial(kernel, n_grp, n_sub), out_shape=(jax.Sh...]
where the time goes in v2:
time: 90.5 us; the launch traced here: 90.2 us
  Pallas kernels  85.1 us (94%)
  local copies, waits for them, and re-layouts  4.45 us (5%)
    pallas_call x1, Pallas kernels, step(): pl.pallas_call(functools.partial(kernel, n_grp, n_sub), out_shape=(jax.Sh...  85.1 us
    unnamed x7, local copies, waits for them, and re-layouts  4.45 us

profile of v2, /device:TPU:1, one launch (start us, length us, event | category | flops | bytes accessed | tf_op | source)
XLA Modules:
  0.0 90.2 jit_solution(9966462417896940838)
XLA Ops:
  0.6 85.1 %shard_map.193 = (bf16[4096,128]{1,0:T(8,128)(2,1)}, bf16[4096,128]{1,0:T(8,128)(2,1)}, f32[7,128,128]{2,1,0:T(8,128)}) custom-call(bf16[4096,128]{1,0:T(8,128)(2,1)} %h_hbm.1, bf16[4096,128]{1,0:T(8,128)(2,1)} %g_hbm.1, bf16[128,128]{1,0:T(8,128)(2,1)} %wfs.1, bf16[128,128]{1,0:T(8,128)(2,1)} %wfo.1, bf16[128,128]{1,0:T(8,128)(2,1)} %wfn.1, ...), custom_call_target="tpu_custom_call" | custom-call | tf_op jit(solution)/shard_map/pallas_call | solution.py:598
  85.7 0.0 copy-start
  85.7 2.4 %copy.24 = bf16[4096,128]{1,0:T(8,128)(2,1)} copy(bf16[4096,128]{1,0:T(8,128)(2,1)} %get-tuple-element.6) | data formatting | bytes 2097152
  88.1 0.0 copy-done
  88.1 0.0 copy-start.1
  88.1 1.0 %copy.25 = bf16[4096,128]{1,0:T(8,128)(2,1)} copy(bf16[4096,128]{1,0:T(8,128)(2,1)S(1)} %copy-done) | data formatting | bytes 2097152
  89.1 0.4 copy-done.1
  89.4 0.8 copy.26
Async XLA Ops:
  85.7 2.4 %copy-start = (bf16[4096,128]{1,0:T(8,128)(2,1)S(1)}, bf16[4096,128]{1,0:T(8,128)(2,1)}, u32[]{:S(2)}) copy-start(bf16[4096,128]{1,0:T(8,128)(2,1)} %get-tuple-element.7) | copy-start | bytes 3145732
  88.1 1.3 %copy-start.1 = (f32[7,128,128]{2,1,0:T(8,128)S(1)}, f32[7,128,128]{2,1,0:T(8,128)}, u32[]{:S(2)}) copy-start(f32[7,128,128]{2,1,0:T(8,128)} %get-tuple-element.8) | copy-start | bytes 1376260

commit v3 on v2

--- a/solution.py
+++ b/solution.py
@@ -120,16 +120,15 @@
     slo_s, shi_s, cslo_s, cshi_s, slo_v, shi_v, cslo_v, cshi_v, owner,
     result_hbm, grad_h_hbm, grad_w,
     h, g, nbr, msk, cnbr, cmsk, result, grad_h,
-    stage, halo_in, halo, far_dfar, farh, own_dsum, cidx, sel, slope, st, summed_down, upd, rowbuf, acc,
+    stage, halo_in, halo, far_dfar, farh, own_dsum, cidx, sel, slope, st, summed, down, upd, rowbuf, acc,
     hist, hist_in, rcnt, gsend, gcore, gchip, gx, gall, tsend, tcore, tchip, tx, cin, cinf, cstaged, cstage, chalo_in, chalo, cown, cfar, cfarh,
     ccidx, csel, yc, dsc, csum, cdown, cdfar, chacc, cback, cback_in, cout, cprol, mm, back, back_in,
-    w_e, rs_e, all_e, w_f, sum_f, rs_f, grp_f, all_f,
+    w_e, rs_e, line_e, all_e, w_f, sum_f, rs_f, line_f, all_f,
     load_s, store_s, halo_ss, halo_rs, hist_ss, hist_rs, gs_ss, gs_rs, ts_ss, ts_rs,
-    ch_ss, ch_rs, cb_ss, cb_rs, bk_ss, bk_rs, e_ss, e_rs, ea_ss, ea_rs, f_ss, f_rs, fg_ss, fg_rs, fa_ss, fa_rs,
+    ch_ss, ch_rs, cb_ss, cb_rs, bk_ss, bk_rs, e_ss, e_rs, el_ss, el_rs, ea_ss, ea_rs, f_ss, f_rs, fl_ss, fl_rs, fa_ss, fa_rs,
 ):
     own, dsum = own_dsum, own_dsum
     far, dfar = far_dfar, far_dfar
-    summed, down = summed_down, summed_down
     gw = rowbuf
     rows = h.shape[0]
     crows = cnbr.shape[1]
@@ -143,6 +142,9 @@
     si = lax.axis_index("sub")
     above = lax.rem(si + 1, n_sub)
     below = lax.rem(si + n_sub - 1, n_sub)
+    core = lax.rem(gi, 2)
+    sibling = gi + 1 - 2 * core
+    other_chip = lax.rem(gi + 2, n_grp)
     has_below = jnp.where(si > 0, 1.0, 0.0).astype(F32)
     has_above = jnp.where(si < n_sub - 1, 1.0, 0.0).astype(F32)
 
@@ -163,45 +165,79 @@
         loads.append(pltpu.make_async_copy(src, dst, load_s.at[k]))
         loads[-1].start()
 
+    plane = n_sub // 2
+    line = lax.rem(si, 2)
+    yz = si // 2
+
+    def in_plane(d):
+        there = lax.rem(yz + d, plane)
+        return there, there * 2 + line
+
     def weights_scatter(array, received, ss, rs):
-        size = array.shape[0] // n_sub
+        size = array.shape[0] // plane
 
         def body(d, carry):
-            there = lax.rem(si + d, n_sub)
-            to_sub(array.at[rows_at(there * size, size)], received.at[rows_at((d - 1) * size, size)], ss, rs, there).start()
+            chunk, there = in_plane(d)
+            to_sub(array.at[rows_at(chunk * size, size)], received.at[rows_at((d - 1) * size, size)], ss, rs, there).start()
             return carry
 
-        lax.fori_loop(1, n_sub, body, 0)
-
-    def weights_sum(array, received, ss, rs):
-        size = array.shape[0] // n_sub
+        lax.fori_loop(1, plane, body, 0)
+
+    def weights_line(array, received, lines, ss, rs, line_ss, line_rs):
+        size = array.shape[0] // plane
         to_sub(received, received, ss, rs, above).wait_recv()
 
         def body(d, total):
             return total + received[rows_at((d - 1) * size, size), :].astype(F32)
 
-        return lax.fori_loop(1, n_sub, body, array[rows_at(si * size, size), :].astype(F32))
-
-    def weights_gather(array, total, ss, rs):
-        size = array.shape[0] // n_sub
-        mine = rows_at(si * size, size)
+        total = lax.fori_loop(1, plane, body, array[rows_at(yz * size, size), :].astype(F32))
+        groups = lines.shape[0] // 2
+        mine = line * groups + (gi if groups > 1 else 0)
+        lines[mine] = total.astype(BF)
+        copies = []
+        for k in range(1, 2 * groups):
+            sub_there = si if k < groups else si + 1 - 2 * line
+            grp_there = lax.rem(gi + k, n_grp) if groups > 1 else gi
+            copies.append(
+                pltpu.make_async_remote_copy(
+                    src_ref=lines.at[mine], dst_ref=lines.at[mine], send_sem=line_ss.at[k - 1], recv_sem=line_rs.at[k - 1],
+                    device_id={"grp": grp_there, "sub": sub_there}, device_id_type=MESH,
+                )
+            )
+            copies[-1].start()
+        return copies
+
+    def weights_gather(array, lines, copies, ss, rs):
+        size = array.shape[0] // plane
+        for c in copies:
+            c.wait_recv()
+        total = lines[0].astype(F32)
+        for k in range(1, lines.shape[0]):
+            total = total + lines[k].astype(F32)
+        mine = rows_at(yz * size, size)
         array[mine, :] = total.astype(BF)
 
         def body(d, carry):
-            to_sub(array.at[mine], array.at[mine], ss, rs, lax.rem(si + d, n_sub)).start()
+            to_sub(array.at[mine], array.at[mine], ss, rs, in_plane(d)[1]).start()
             return carry
 
-        lax.fori_loop(1, n_sub, body, 0)
+        lax.fori_loop(1, plane, body, 0)
 
     barrier = pltpu.get_barrier_semaphore()
 
-    def greet(d, carry):
-        pl.semaphore_signal(barrier, inc=1, device_id={"sub": lax.rem(si + d, n_sub)}, device_id_type=MESH)
-        return carry
-
-    lax.fori_loop(1, n_sub, greet, 0)
-    for d in range(1, n_grp):
-        pl.semaphore_signal(barrier, inc=1, device_id={"grp": lax.rem(gi + d, n_grp)}, device_id_type=MESH)
+    def greet(sub_there, grp_there):
+        pl.semaphore_signal(barrier, inc=1, device_id={"grp": grp_there, "sub": sub_there}, device_id_type=MESH)
+
+    def greet_plane(d, carry):
+        greet(in_plane(d)[1], gi)
+        return carry
+
+    lax.fori_loop(1, plane, greet_plane, 0)
+    for k in range(1, 2 * n_grp):
+        greet(si if k < n_grp else si + 1 - 2 * line, lax.rem(gi + k, n_grp))
+    for there in (above, below):
+        greet(there, gi)
+        greet(there, sibling)
 
     def widen(i, carry):
         upd[rows_at(i * TILE, TILE), :] = h[rows_at(i * TILE, TILE), :].astype(F32)
@@ -212,7 +248,7 @@
     gather_rows(shi_s, upd, rowbuf, 0, halo_rows)
     gather_rows(slo_s, upd, rowbuf, halo_rows, halo_rows)
     stage[...] = rowbuf[0 : 2 * halo_rows, :].astype(BF)
-    pl.semaphore_wait(barrier, n_sub - 1 + n_grp - 1)
+    pl.semaphore_wait(barrier, plane - 1 + 2 * n_grp - 1 + 4)
     half = halo_rows // 2
     halo_copies = []
     for c in range(4):
@@ -246,16 +282,13 @@
         )
         hist_copies[-1].start()
 
-    core = lax.rem(gi, 2)
-    sibling = gi + 1 - 2 * core
-    other_chip = lax.rem(gi + 2, n_grp)
     part_rows = crows // 2
     mine = rows_at(core * part_rows, part_rows)
     theirs = rows_at((1 - core) * part_rows, part_rows)
 
     def group_first(sums, send, received, ss, rs):
-        send[...] = sums[...].astype(BF)
-        copy = to_grp(send.at[theirs], received, ss.at[0], rs.at[0], sibling)
+        send[...] = sums[theirs, :].astype(BF)
+        copy = to_grp(send, received, ss.at[0], rs.at[0], sibling)
         copy.start()
         return [copy]
 
@@ -316,11 +349,14 @@
             slope[b] = q
             summed[rows_at(b * BLK, BLK), :] = total.astype(BF)
 
-    def forward_update(i):
+    def forward_new(i):
         part = rows_at(i * TILE, TILE)
         new = h[part, :].astype(F32) + dot(summed[part, :], wfn[...])
         upd[part, :] = new
-        acc[...] += dot(st[i], new.astype(BF))
+        return new.astype(BF)
+
+    def forward_update(i):
+        acc[...] += dot(st[i], forward_new(i))
 
     def forward_tiles(p, carry):
         forward_update(p * 2 - 2)
@@ -332,11 +368,12 @@
     forward_edges(0)
     forward_edges(1)
     lax.fori_loop(1, tiles // 2, forward_tiles, 0)
-    forward_update(tiles - 2)
-    forward_update(tiles - 1)
-
+    new_a, new_b = forward_new(tiles - 2), forward_new(tiles - 1)
+    acc[theirs, :] += dot(st[tiles - 2, theirs, :], new_a) + dot(st[tiles - 1, theirs, :], new_b)
+
+    t_copies = group_first(acc, tsend, tcore, ts_ss, ts_rs)
+    acc[mine, :] += dot(st[tiles - 2, mine, :], new_a) + dot(st[tiles - 1, mine, :], new_b)
     group_third(g_copies, gchip, gx, None, gall, gs_ss, gs_rs)
-    t_copies = group_first(acc, tsend, tcore, ts_ss, ts_rs)
     for c in hist_copies:
         c.wait_recv()
     counts = hist[...]
@@ -353,17 +390,22 @@
     dsc[...] = (dot(yc[...].astype(BF), wcn[...], 1, 1) * 0.5).astype(BF)
     build_selectors(ccidx, csel, cblocks)
     group_third(t_copies, tchip, tx, rcnt, cin, ts_ss, ts_rs)
-    t_copies[2].wait_recv()
-
-    cinf[...] = cin[...].astype(F32)
+    cinf[mine, :] = cin[mine, :].astype(F32)
+    cinf[theirs, :] = jnp.zeros((part_rows, D), F32)
     gather_rows(cshi_s, cinf, cstaged, 0, chalo_rows)
     gather_rows(cslo_s, cinf, cstaged, chalo_rows, chalo_rows)
     cstage[...] = cstaged[...].astype(BF)
     ch_copies = []
-    for c in range(2):
-        part = pl.ds(c * chalo_rows, chalo_rows)
-        ch_copies.append(to_sub(cstage.at[part], chalo_in.at[part], ch_ss.at[c], ch_rs.at[c], (above, below)[c]))
+    for c in range(4):
+        part = pl.ds((c // 2) * chalo_rows, chalo_rows)
+        ch_copies.append(
+            pltpu.make_async_remote_copy(
+                src_ref=cstage.at[part], dst_ref=chalo_in.at[c % 2, part], send_sem=ch_ss.at[c], recv_sem=ch_rs.at[c],
+                device_id={"grp": (gi, sibling)[c % 2], "sub": (above, below)[c // 2]}, device_id_type=MESH,
+            )
+        )
         ch_copies[-1].start()
+    t_copies[2].wait_recv()
     r = dot(cin[...], jnp.concatenate([wcs[...] * 0.5, wco[...] * 0.5], axis=1))
     cown[...] = r[:, :D].astype(BF)
     cfar[...] = r[:, D:].astype(BF)
@@ -376,8 +418,9 @@
     lax.fori_loop(0, tiles, known_part, 0)
     for c in ch_copies:
         c.wait_recv()
-    chalo[0:chalo_rows, :] = (chalo_in[0:chalo_rows, :].astype(F32) * has_below).astype(BF)
-    chalo[chalo_rows:, :] = (chalo_in[chalo_rows:, :].astype(F32) * has_above).astype(BF)
+    arrived = chalo_in[0].astype(F32) + chalo_in[1].astype(F32)
+    chalo[0:chalo_rows, :] = (arrived[0:chalo_rows] * has_below).astype(BF)
+    chalo[chalo_rows:, :] = (arrived[chalo_rows:] * has_above).astype(BF)
     cfarh[...] = dot(chalo[...], wco[...] * 0.5).astype(BF)
     chacc[...] = jnp.zeros_like(chacc)
 
@@ -405,8 +448,10 @@
 
     cout[...] = (cin[...].astype(F32) + dot(csum[...], wcn[...])).astype(BF)
     cprol[...] = dot(cout[...], wpr[...]).astype(BF)
-    w_e[0:128, :] = dot(cin[...], cdown[...], 0, 0).astype(BF)
-    w_e[128:256, :] = (dot(cin[...], cdfar[...].astype(BF), 0, 0) + dot(chalo[...], cback[...], 0, 0)).astype(BF)
+
+    r = dot(cin[...], jnp.concatenate([cdown[...], cdfar[...].astype(BF)], axis=1), 0, 0)
+    w_e[0:128, :] = r[:, :D].astype(BF)
+    w_e[128:256, :] = (r[:, D:] + dot(chalo[...], cback[...], 0, 0)).astype(BF)
     w_e[256:384, :] = dot(csum[...], yc[...].astype(BF), 0, 0).astype(BF)
     w_e[384:512, :] = dot(cout[...], gall[...], 0, 0).astype(BF)
     weights_scatter(w_e, rs_e, e_ss, e_rs)
@@ -432,7 +477,6 @@
     m = (dcin * rcnt[...]).astype(BF)
     mm[:, :D] = m
     mm[:, D:] = (dot(m, wfn[...], 1, 1) * 0.5).astype(BF)
-    weights_gather(all_e, weights_sum(w_e, rs_e, e_ss, e_rs), ea_ss, ea_rs)
 
     sum_f[...] = jnp.zeros_like(sum_f)
 
@@ -444,10 +488,11 @@
             y = g[part, :].astype(F32) + r[:, :D]
             upd[part, :] = y
             dsum[part, :] = (gw[part, :] + r[:, D:]).astype(BF)
-            sum_f[256:384, :] += dot(summed[part, :], y.astype(BF), 0, 0)
         return carry
 
     lax.fori_loop(0, tiles // 2, cotangents, 0)
+
+    e_copies = weights_line(w_e, rs_e, line_e, e_ss, e_rs, el_ss, el_rs)
 
     bk_copies = []
     for c in range(2 * hblocks):
@@ -471,33 +516,41 @@
             part = rows_at(c * BLK, BLK)
             to_sub(back.at[part], back_in.at[part], bk_ss.at[c], bk_rs.at[c], there).start()
 
-    def backward_dense(hb):
+    def backward_weights(hb):
         parts = [rows_at((u * hblocks + hb) * BLK, BLK) for u in range(blocks // hblocks)]
         grads = jnp.concatenate([jnp.concatenate([down[p, :], dfar[p, :]], axis=1) for p in parts], axis=0)
         r = dot(jnp.concatenate([h[p, :] for p in parts], axis=0), grads, 0, 0)
+        below_part = rows_at(hb * BLK, BLK)
+        above_part = rows_at(halo_rows + hb * BLK, BLK)
+        halo_grad = jnp.concatenate([back[below_part, :], back[above_part, :]], axis=0)
+        halo_row = jnp.concatenate([halo[below_part, :], halo[above_part, :]], axis=0)
         sum_f[0:128, :] += r[:, :D]
-        sum_f[128:256, :] += r[:, D:]
-        r = dot(grads, jnp.concatenate([wfs[...], wfo[...]], axis=1), 1, 1)
+        sum_f[128:256, :] += r[:, D:] + dot(halo_row, halo_grad, 0, 0)
+        y = jnp.concatenate([upd[p, :] for p in parts], axis=0)
+        sum_f[256:384, :] += dot(jnp.concatenate([summed[p, :] for p in parts], axis=0), y.astype(BF), 0, 0)
+        return parts, grads, y
+
+    def backward_latents(parts, grads, y):
+        r = dot(grads, jnp.concatenate([wfs[...], wfo[...]], axis=1), 1, 1) + y
         for u, p in enumerate(parts):
-            upd[p, :] += r[u * BLK : (u + 1) * BLK]
+            upd[p, :] = r[u * BLK : (u + 1) * BLK]
 
     def backward_step(hb, carry):
-        backward_dense(hb - 1)
+        backward_latents(*backward_weights(hb - 1))
         backward_edges(hb)
         return carry
 
     backward_edges(0)
     lax.fori_loop(1, hblocks, backward_step, 0)
-    sum_f[128:256, :] += dot(halo[...], back[...], 0, 0)
-    backward_dense(hblocks - 1)
+    last = backward_weights(hblocks - 1)
     w_f[...] = sum_f[...].astype(BF)
     weights_scatter(w_f, rs_f, f_ss, f_rs)
-
-    grp_f[gi] = weights_sum(w_f, rs_f, f_ss, f_rs)
-    fg_copies = []
-    for d in range(1, n_grp):
-        fg_copies.append(to_grp(grp_f.at[gi], grp_f.at[gi], fg_ss.at[d - 1], fg_rs.at[d - 1], lax.rem(gi + d, n_grp)))
-        fg_copies[-1].start()
+    weights_gather(all_e, line_e, e_copies, ea_ss, ea_rs)
+    backward_latents(*last)
+
+
+    f_copies = weights_line(w_f, rs_f, line_f, f_ss, f_rs, fl_ss, fl_rs)
+
     for c in bk_copies:
         c.wait_recv()
     halo[0:halo_rows, :] = (dot(back_in[0:halo_rows, :], wfo[...], 1, 1) * has_above).astype(BF)
@@ -516,36 +569,36 @@
         grad_h[part, :] = (upd[part, :] + dot(jnp.concatenate(hots, axis=0), halo[...])).astype(BF)
         return carry
 
+    def store_half(k):
+        part = pl.ds(k * (rows // 2), rows // 2)
+        stores.append(pltpu.make_async_copy(grad_h.at[part], grad_h_hbm.at[part], store_s.at[1 + k]))
+        stores[-1].start()
+
     lax.fori_loop(0, rows // group // 2, returned, 0)
-    for c in fg_copies:
-        c.wait_recv()
-    total = grp_f[0]
-    for k in range(1, n_grp):
-        total = total + grp_f[k]
-    weights_gather(all_f, total, fa_ss, fa_rs)
+    store_half(0)
+    weights_gather(all_f, line_f, f_copies, fa_ss, fa_rs)
     lax.fori_loop(rows // group // 2, rows // group, returned, 0)
-    stores.append(pltpu.make_async_copy(grad_h, grad_h_hbm, store_s.at[1]))
-    stores[1].start()
+    store_half(1)
 
     def finish(array, ss, rs, first, count):
-        size = array.shape[0] // n_sub
+        size = array.shape[0] // plane
         others = array.at[pl.ds(0, array.shape[0] - size)]
         to_sub(others, others, ss, rs, above).wait_recv()
         for k in range(count):
             grad_w[first + k] = array[k * 128 : (k + 1) * 128, :].astype(F32)
 
+    finish(all_f, fa_ss, fa_rs, 0, 3)
     finish(all_e, ea_ss, ea_rs, 3, 4)
-    finish(all_f, fa_ss, fa_rs, 0, 3)
 
     for c in halo_copies + hist_copies + g_copies + t_copies + ch_copies + cb_copies:
         c.wait_send()
-    for c in bk_copies + fg_copies:
+    for c in bk_copies + f_copies + e_copies:
         c.wait_send()
     for c in stores:
         c.wait()
     for received, array, ss, gather_ss, rs in ((rs_e, all_e, e_ss, ea_ss, e_rs), (rs_f, all_f, f_ss, fa_ss, f_rs)):
         to_sub(received, received, ss, rs, above).wait_send()
-        others = array.at[pl.ds(0, array.shape[0] - array.shape[0] // n_sub)]
+        others = array.at[pl.ds(0, array.shape[0] - array.shape[0] // plane)]
         to_sub(others, others, gather_ss, rs, above).wait_send()
 
 
@@ -566,7 +619,7 @@
     V = pltpu.VMEM
     dma = pltpu.SemaphoreType.DMA
     w_rows = 4 * D
-    wc = w_rows // n_sub
+    wc = w_rows // (n_sub // 2)
     i32 = jnp.int32
     scratch = [
         V((rows, D), BF), V((rows, D), BF), V((slots, rows), i32), V((slots, rows), i32),
@@ -575,25 +628,25 @@
         V((rows, D), BF), V((2 * halo, D), BF), V((rows, D), BF),
         V((blocks, 8, 128), F32), V((blocks, 4 * BLK, edges), BF), V((blocks, edges, D), BF),
         V((rows // TILE, crows, TILE), BF),
-        V((rows, D), BF), V((rows, D), F32), V((rows, D), F32), V((crows, D), F32),
+        V((rows, D), BF), V((rows, D), BF), V((rows, D), F32), V((rows, D), F32), V((crows, D), F32),
         V((16, 128), F32), V((n_grp - 1, 16, 128), F32), V((crows, D), F32),
-        V((crows, D), BF), V((crows // 2, D), BF), V((crows // 2, D), BF), V((crows // 2, D), BF), V((crows, D), BF),
-        V((crows, D), BF), V((crows // 2, D), BF), V((crows // 2, D), BF), V((crows // 2, D), BF), V((crows, D), BF),
-        V((crows, D), F32), V((2 * chalo, D), F32), V((2 * chalo, D), BF), V((2 * chalo, D), BF), V((2 * chalo, D), BF),
+        V((crows // 2, D), BF), V((crows // 2, D), BF), V((crows // 2, D), BF), V((crows // 2, D), BF), V((crows, D), BF),
+        V((crows // 2, D), BF), V((crows // 2, D), BF), V((crows // 2, D), BF), V((crows // 2, D), BF), V((crows, D), BF),
+        V((crows, D), F32), V((2 * chalo, D), F32), V((2 * chalo, D), BF), V((2, 2 * chalo, D), BF), V((2 * chalo, D), BF),
         V((crows, D), BF), V((crows, D), BF), V((2 * chalo, D), BF),
         V((cblocks, 8, 128), F32), V((cblocks, 4 * BLK, edges), BF),
         V((crows, D), F32), V((crows, D), BF), V((crows, D), BF), V((crows, D), BF), V((crows, D), F32),
         V((2 * chalo, D), F32), V((2 * chalo, D), BF), V((2 * chalo, D), BF),
         V((crows, D), BF), V((crows, D), BF), V((crows, 2 * D), BF),
         V((2 * halo, D), BF), V((2 * halo, D), BF),
-        V((w_rows, D), BF), V((w_rows - wc, D), BF), V((w_rows, D), BF),
-        V((w_rows, D), BF), V((w_rows, D), F32), V((w_rows - wc, D), BF), V((n_grp, wc, D), F32), V((w_rows, D), BF),
-        dma((6,)), dma((2,)), dma((4,)), dma((4,)),
+        V((w_rows, D), BF), V((w_rows - wc, D), BF), V((2, wc, D), BF), V((w_rows, D), BF),
+        V((w_rows, D), BF), V((w_rows, D), F32), V((w_rows - wc, D), BF), V((2 * n_grp, wc, D), BF), V((w_rows, D), BF),
+        dma((6,)), dma((3,)), dma((4,)), dma((4,)),
         dma((n_grp - 1,)), dma((n_grp - 1,)), dma((3,)), dma((3,)), dma((3,)), dma((3,)),
-        dma((2,)), dma((2,)), dma((2,)), dma((2,)),
+        dma((4,)), dma((4,)), dma((2,)), dma((2,)),
         dma((2 * halo // BLK,)), dma((2 * halo // BLK,)),
-        dma, dma, dma, dma,
-        dma, dma, dma((n_grp - 1,)), dma((n_grp - 1,)), dma, dma,
+        dma, dma, dma((1,)), dma((1,)), dma, dma,
+        dma, dma, dma((2 * n_grp - 1,)), dma((2 * n_grp - 1,)), dma, dma,
     ]
     outs = pl.pallas_call(
         functools.partial(kernel, n_grp, n_sub),

time: 90.5 us -> 83.3 us (0.920)
  Pallas kernels: 85.1 us -> 77.9 us
    pallas_call x1, Pallas kernels: 85.1 us -> 77.9 us  [step(): pl.pallas_call(functools.partial(kernel, n_grp, n_sub), out_shape=(jax.Sh...]
where the time goes in v3:
time: 83.3 us; the launch traced here: 83 us
  Pallas kernels  77.9 us (94%)
  local copies, waits for them, and re-layouts  4.45 us (5%)
    pallas_call x1, Pallas kernels, step(): pl.pallas_call(functools.partial(kernel, n_grp, n_sub), out_shape=(jax.Sh...  77.9 us
    unnamed x7, local copies, waits for them, and re-layouts  4.45 us

profile of v3, /device:TPU:1, one launch (start us, length us, event | category | flops | bytes accessed | tf_op | source)
XLA Modules:
  0.0 83.0 jit_solution(382174255439938616)
XLA Ops:
  0.6 77.9 %shard_map.193 = (bf16[4096,128]{1,0:T(8,128)(2,1)}, bf16[4096,128]{1,0:T(8,128)(2,1)}, f32[7,128,128]{2,1,0:T(8,128)}) custom-call(bf16[4096,128]{1,0:T(8,128)(2,1)} %h_hbm.1, bf16[4096,128]{1,0:T(8,128)(2,1)} %g_hbm.1, bf16[128,128]{1,0:T(8,128)(2,1)} %wfs.1, bf16[128,128]{1,0:T(8,128)(2,1)} %wfo.1, bf16[128,128]{1,0:T(8,128)(2,1)} %wfn.1, ...), custom_call_target="tpu_custom_call" | custom-call | tf_op jit(solution)/shard_map/pallas_call | solution.py:651
  78.5 0.0 copy-start
  78.5 2.4 %copy.24 = bf16[4096,128]{1,0:T(8,128)(2,1)} copy(bf16[4096,128]{1,0:T(8,128)(2,1)} %get-tuple-element.6) | data formatting | bytes 2097152
  80.9 0.0 copy-done
  80.9 0.0 copy-start.1
  80.9 1.0 %copy.25 = bf16[4096,128]{1,0:T(8,128)(2,1)} copy(bf16[4096,128]{1,0:T(8,128)(2,1)S(1)} %copy-done) | data formatting | bytes 2097152
  81.9 0.4 copy-done.1
  82.2 0.8 copy.26
Async XLA Ops:
  78.5 2.4 %copy-start = (bf16[4096,128]{1,0:T(8,128)(2,1)S(1)}, bf16[4096,128]{1,0:T(8,128)(2,1)}, u32[]{:S(2)}) copy-start(bf16[4096,128]{1,0:T(8,128)(2,1)} %get-tuple-element.7) | copy-start | bytes 3145732
  80.9 1.3 %copy-start.1 = (f32[7,128,128]{2,1,0:T(8,128)S(1)}, f32[7,128,128]{2,1,0:T(8,128)}, u32[]{:S(2)}) copy-start(f32[7,128,128]{2,1,0:T(8,128)} %get-tuple-element.8) | copy-start | bytes 1376260

commit v4 on v3

--- a/solution.py
+++ b/solution.py
@@ -114,11 +114,33 @@
     return dot(sel, grad)
 
 
+def copy_kernel(*refs):
+    count = len(refs) // 2
+    for k in range(count):
+        refs[count + k][...] = refs[k][...].astype(refs[count + k].dtype)
+
+
+def copied(arrays, steps):
+    specs = []
+    for a in arrays:
+        if a.ndim == 2:
+            specs.append(pl.BlockSpec((a.shape[0] // steps, a.shape[1]), lambda i: (i, 0)))
+        else:
+            specs.append(pl.BlockSpec((a.shape[0], a.shape[1] // steps, a.shape[2]), lambda i: (0, i, 0)))
+    return pl.pallas_call(
+        copy_kernel,
+        grid=(steps,),
+        out_shape=tuple(jax.ShapeDtypeStruct(a.shape, BF if a.ndim == 2 else F32) for a in arrays),
+        in_specs=specs,
+        out_specs=tuple(specs),
+    )(*arrays)
+
+
 def kernel(
     n_grp, n_sub,
     h_hbm, g_hbm, wfs, wfo, wfn, wcs, wco, wcn, wpr, nbr_hbm, msk_hbm, cnbr_hbm, cmsk_hbm,
     slo_s, shi_s, cslo_s, cshi_s, slo_v, shi_v, cslo_v, cshi_v, owner,
-    result_hbm, grad_h_hbm, grad_w,
+    result_hbm, grad_h_hbm, grad_w_hbm,
     h, g, nbr, msk, cnbr, cmsk, result, grad_h,
     stage, halo_in, halo, far_dfar, farh, own_dsum, cidx, sel, slope, st, summed, down, upd, rowbuf, acc,
     hist, hist_in, rcnt, gsend, gcore, gchip, gx, gall, tsend, tcore, tchip, tx, cin, cinf, cstaged, cstage, chalo_in, chalo, cown, cfar, cfarh,
@@ -426,8 +448,8 @@
 
     def mid_blocks(p, carry):
         both = None
-        for u in range(8):
-            b = p * 8 + u
+        for u in range(16):
+            b = p * 16 + u
             part = rows_at(b * BLK, BLK)
             total, q = edge_forward(csel[b], jnp.concatenate([cfar[part, :], cfarh[...], cown[part, :]], axis=0))
             csum[part, :] = total.astype(BF)
@@ -438,7 +460,7 @@
         chacc[...] += both
         return carry
 
-    lax.fori_loop(0, cblocks // 8, mid_blocks, 0)
+    lax.fori_loop(0, cblocks // 16, mid_blocks, 0)
     cback[...] = chacc[...].astype(BF)
     cb_copies = []
     for c in range(2):
@@ -457,13 +479,13 @@
     weights_scatter(w_e, rs_e, e_ss, e_rs)
 
     def prolonged(p, carry):
-        for u in range(2):
-            i = p * 2 + u
+        for u in range(4):
+            i = p * 4 + u
             part = rows_at(i * TILE, TILE)
             result[part, :] = (upd[part, :] + dot(st[i], cprol[...], 0, 0)).astype(BF)
         return carry
 
-    lax.fori_loop(0, tiles // 2, prolonged, 0)
+    lax.fori_loop(0, tiles // 4, prolonged, 0)
     stores = [pltpu.make_async_copy(result, result_hbm, store_s.at[0])]
     stores[0].start()
     for c in cb_copies:
@@ -481,8 +503,8 @@
     sum_f[...] = jnp.zeros_like(sum_f)
 
     def cotangents(p, carry):
-        for u in range(2):
-            i = p * 2 + u
+        for u in range(4):
+            i = p * 4 + u
             part = rows_at(i * TILE, TILE)
             r = dot(st[i], mm[...], 0, 0)
             y = g[part, :].astype(F32) + r[:, :D]
@@ -490,7 +512,7 @@
             dsum[part, :] = (gw[part, :] + r[:, D:]).astype(BF)
         return carry
 
-    lax.fori_loop(0, tiles // 2, cotangents, 0)
+    lax.fori_loop(0, tiles // 4, cotangents, 0)
 
     e_copies = weights_line(w_e, rs_e, line_e, e_ss, e_rs, el_ss, el_rs)
 
@@ -580,15 +602,17 @@
     lax.fori_loop(rows // group // 2, rows // group, returned, 0)
     store_half(1)
 
-    def finish(array, ss, rs, first, count):
+    def finish(array, ss, rs, first, count, sem):
         size = array.shape[0] // plane
         others = array.at[pl.ds(0, array.shape[0] - size)]
         to_sub(others, others, ss, rs, above).wait_recv()
-        for k in range(count):
-            grad_w[first + k] = array[k * 128 : (k + 1) * 128, :].astype(F32)
-
-    finish(all_f, fa_ss, fa_rs, 0, 3)
-    finish(all_e, ea_ss, ea_rs, 3, 4)
+        stores.append(
+            pltpu.make_async_copy(array.at[pl.ds(0, count * D)], grad_w_hbm.at[pl.ds(first * D, count * D)], sem)
+        )
+        stores[-1].start()
+
+    finish(all_e, ea_ss, ea_rs, 3, 4, store_s.at[3])
+    finish(all_f, fa_ss, fa_rs, 0, 3, store_s.at[4])
 
     for c in halo_copies + hist_copies + g_copies + t_copies + ch_copies + cb_copies:
         c.wait_send()
@@ -641,7 +665,7 @@
         V((2 * halo, D), BF), V((2 * halo, D), BF),
         V((w_rows, D), BF), V((w_rows - wc, D), BF), V((2, wc, D), BF), V((w_rows, D), BF),
         V((w_rows, D), BF), V((w_rows, D), F32), V((w_rows - wc, D), BF), V((2 * n_grp, wc, D), BF), V((w_rows, D), BF),
-        dma((6,)), dma((3,)), dma((4,)), dma((4,)),
+        dma((6,)), dma((5,)), dma((4,)), dma((4,)),
         dma((n_grp - 1,)), dma((n_grp - 1,)), dma((3,)), dma((3,)), dma((3,)), dma((3,)),
         dma((4,)), dma((4,)), dma((2,)), dma((2,)),
         dma((2 * halo // BLK,)), dma((2 * halo // BLK,)),
@@ -653,13 +677,13 @@
         out_shape=(
             jax.ShapeDtypeStruct((rows, D), BF),
             jax.ShapeDtypeStruct((rows, D), BF),
-            jax.ShapeDtypeStruct((7, D, D), F32),
+            jax.ShapeDtypeStruct((7 * D, D), BF),
         ),
         in_specs=[hbm] * 2 + [vmem] * 7 + [hbm] * 4 + [smem] * 4 + [vmem] * 5,
-        out_specs=(hbm, hbm, vmem),
+        out_specs=(hbm, hbm, hbm),
         scratch_shapes=scratch,
         compiler_params=pltpu.CompilerParams(
-            collective_id=0, has_side_effects=True, vmem_limit_bytes=63 * 1024 * 1024
+            collective_id=0, has_side_effects=True, vmem_limit_bytes=60 * 1024 * 1024 + 512 * 1024
         ),
     )(
         states, cotangent, fine_self, fine_other, fine_node, coarse_self, coarse_other, coarse_node, prolong,
@@ -669,7 +693,7 @@
         coarse_send_lo.reshape(1, -1), coarse_send_hi.reshape(1, -1),
         coarse_owner.reshape(-1, 128),
     )
-    return outs
+    return copied((outs[0], outs[1], outs[2].reshape(7, D, D)), 2)
 
 
 def solution(mesh):

time: 83.3 us -> 80.3 us (0.964)
  local copies, waits for them, and re-layouts: 4.45 us -> 0 us
  Pallas kernels: 77.9 us -> 79.4 us
    unnamed x7 -> x0, local copies, waits for them, and re-layouts: 4.45 us -> none
    pallas_call x0 -> x1, Pallas kernels: none -> 2.76 us  [copied(): pl.pallas_call(copy_kernel, grid=(steps,), out_shape=tuple((jax.ShapeDtyp...]
    pallas_call x1, Pallas kernels: 77.9 us -> 76.7 us  [step(): pl.pallas_call(functools.partial(kernel, n_grp, n_sub), out_shape=(jax.Sh...]
where the time goes in v4:
time: 80.3 us; the launch traced here: 80.1 us
  Pallas kernels  79.4 us (99%)
    pallas_call x1, Pallas kernels, step(): pl.pallas_call(functools.partial(kernel, n_grp, n_sub), out_shape=(jax.Sh...  76.7 us
    pallas_call x1, Pallas kernels, copied(): pl.pallas_call(copy_kernel, grid=(steps,), out_shape=tuple((jax.ShapeDtyp...  2.76 us

profile of v4, /device:TPU:1, one launch (start us, length us, event | category | flops | bytes accessed | tf_op | source)
XLA Modules:
  0.0 80.1 jit_solution(8027147037164743812)
XLA Ops:
  0.6 76.7 %shard_map.193 = (bf16[4096,128]{1,0:T(8,128)(2,1)}, bf16[4096,128]{1,0:T(8,128)(2,1)}, bf16[896,128]{1,0:T(8,128)(2,1)}) custom-call(bf16[4096,128]{1,0:T(8,128)(2,1)} %h_hbm.1, bf16[4096,128]{1,0:T(8,128)(2,1)} %g_hbm.1, bf16[128,128]{1,0:T(8,128)(2,1)} %wfs.1, bf16[128,128]{1,0:T(8,128)(2,1)} %wfo.1, bf16[128,128]{1,0:T(8,128)(2,1)} %wfn.1, ...), custom_call_target="tpu_custom_call" | custom-call | tf_op jit(solution)/shard_map/pallas_call | solution.py:675
  77.3 2.8 %shard_map.194 = (bf16[4096,128]{1,0:T(8,128)(2,1)}, bf16[4096,128]{1,0:T(8,128)(2,1)}, f32[7,128,128]{2,1,0:T(8,128)}) custom-call(bf16[4096,128]{1,0:T(8,128)(2,1)} %get-tuple-element.6.refs_0_, bf16[4096,128]{1,0:T(8,128)(2,1)} %get-tuple-element.7.refs_1_, bf16[7,128,128]{2,1,0:T(8,128)(2,1)} %bitcast.10), custom_call_target="tpu_custom_call" | custom-call | tf_op jit(solution)/shard_map/pallas_call | solution.py:130

commit v5 on v4

--- a/solution.py
+++ b/solution.py
@@ -396,6 +396,7 @@
     t_copies = group_first(acc, tsend, tcore, ts_ss, ts_rs)
     acc[mine, :] += dot(st[tiles - 2, mine, :], new_a) + dot(st[tiles - 1, mine, :], new_b)
     group_third(g_copies, gchip, gx, None, gall, gs_ss, gs_rs)
+    group_second(t_copies, acc, tcore, tchip, tx, ts_ss, ts_rs)
     for c in hist_copies:
         c.wait_recv()
     counts = hist[...]
@@ -408,7 +409,6 @@
     prepare_slots(cnbr, cmsk, ccidx, crows, chalo_rows, 1)
     g_copies[2].wait_recv()
     yc[...] = dot(gall[...], wpr[...], 1, 1)
-    group_second(t_copies, acc, tcore, tchip, tx, ts_ss, ts_rs)
     dsc[...] = (dot(yc[...].astype(BF), wcn[...], 1, 1) * 0.5).astype(BF)
     build_selectors(ccidx, csel, cblocks)
     group_third(t_copies, tchip, tx, rcnt, cin, ts_ss, ts_rs)
@@ -567,11 +567,11 @@
     last = backward_weights(hblocks - 1)
     w_f[...] = sum_f[...].astype(BF)
     weights_scatter(w_f, rs_f, f_ss, f_rs)
+    backward_latents(*last)
+
+
+    f_copies = weights_line(w_f, rs_f, line_f, f_ss, f_rs, fl_ss, fl_rs)
     weights_gather(all_e, line_e, e_copies, ea_ss, ea_rs)
-    backward_latents(*last)
-
-
-    f_copies = weights_line(w_f, rs_f, line_f, f_ss, f_rs, fl_ss, fl_rs)
 
     for c in bk_copies:
         c.wait_recv()

time: 80.3 us -> 79.7 us (level)
  no operation moved by 1% of the time
where the time goes in v5:
time: 79.7 us; the launch traced here: 79.4 us
  Pallas kernels  78.8 us (99%)
    pallas_call x1, Pallas kernels, step(): pl.pallas_call(functools.partial(kernel, n_grp, n_sub), out_shape=(jax.Sh...  76 us
    pallas_call x1, Pallas kernels, copied(): pl.pallas_call(copy_kernel, grid=(steps,), out_shape=tuple((jax.ShapeDtyp...  2.76 us

profile of v5, /device:TPU:1, one launch (start us, length us, event | category | flops | bytes accessed | tf_op | source)
XLA Modules:
  0.0 79.4 jit_solution(12734456754984789948)
XLA Ops:
  0.6 76.0 %shard_map.193 = (bf16[4096,128]{1,0:T(8,128)(2,1)}, bf16[4096,128]{1,0:T(8,128)(2,1)}, bf16[896,128]{1,0:T(8,128)(2,1)}) custom-call(bf16[4096,128]{1,0:T(8,128)(2,1)} %h_hbm.1, bf16[4096,128]{1,0:T(8,128)(2,1)} %g_hbm.1, bf16[128,128]{1,0:T(8,128)(2,1)} %wfs.1, bf16[128,128]{1,0:T(8,128)(2,1)} %wfo.1, bf16[128,128]{1,0:T(8,128)(2,1)} %wfn.1, ...), custom_call_target="tpu_custom_call" | custom-call | tf_op jit(solution)/shard_map/pallas_call | solution.py:675
  76.7 2.8 %shard_map.194 = (bf16[4096,128]{1,0:T(8,128)(2,1)}, bf16[4096,128]{1,0:T(8,128)(2,1)}, f32[7,128,128]{2,1,0:T(8,128)}) custom-call(bf16[4096,128]{1,0:T(8,128)(2,1)} %get-tuple-element.6.refs_0_, bf16[4096,128]{1,0:T(8,128)(2,1)} %get-tuple-element.7.refs_1_, bf16[7,128,128]{2,1,0:T(8,128)(2,1)} %bitcast.10), custom_call_target="tpu_custom_call" | custom-call | tf_op jit(solution)/shard_map/pallas_call | solution.py:130
